TPU v7x, 512 devices: a whole 4x8x8 slice. The times are simulated.
512 devices in a mesh: phi: 128 (over x, y_hi, z, core), eta: 4 (over y_lo).
Axes of the slice: x: 4, y: 8 (y_hi: 2, y_lo: 4; y = y_hi * 4 + y_lo), z: 8, core: 2. Of those that a mesh axis runs over, the one named last changes fastest.
Arguments:
- noisy_field: bfloat16 [512, 256, 768], P('phi', 'eta'), may hold values from -6 to 6
- noise_draw: bfloat16 [512, 256, 768], P('phi', 'eta'), may hold values from -6 to 6
- coarse_latent: bfloat16 [2048, 512], P('phi'), may hold values from -6 to 6
- particle_type: int32 [2048], P('phi'), may hold values from 0 to 7
- type_table: bfloat16 [8, 512], replicated, may hold values from -6 to 6
- kv_weight: bfloat16 [512, 384], replicated, may hold values from -2.3864854 to 2.3864854
- norm_gain: float32 [2, 96], replicated, may hold values from 0.1 to 1.9
- conv_weight: bfloat16 [2, 9, 96, 96], replicated, may hold values from -0.21875 to 0.21875
- query_weight: bfloat16 [2, 96, 96], replicated, may hold values from -0.625 to 0.625
- mix_weight: bfloat16 [2, 96, 96], replicated, may hold values from -0.625 to 0.625
- out_weight: bfloat16 [2, 96, 96], replicated, may hold values from -0.15625 to 0.15625
Outputs:
- denoised: bfloat16 [512, 256, 768], P('phi', 'eta')
All inputs are finite; a program needn't handle non-finite values.
Results may differ from a plain program's by a relative error of at most 0.0067.
Values may be sent and summed in bfloat16 or wider, within the bound.
No kernel may reach another device: no remote copies, remote signals or barrier semaphores. Data moves between devices by JAX's collectives and lax.ppermute only.
A program may use at most 64 MiB of HBM per device.

v0:
```python
import math

import jax
import jax.numpy as jnp
from jax import lax
from jax.sharding import PartitionSpec as P

C = 96
TYPES = 8
HEADS = 2
BLOCKS = 2
LAYERS = 8
HDIM = 48


eps = 1e-06


def padded_2(cells, sides, width, closed):
    for axis, dim in sides:
        count = lax.axis_size(axis)
        ends = count if closed else count - 1
        head = lax.slice_in_dim(cells, 0, width, axis=dim)
        tail = lax.slice_in_dim(cells, cells.shape[dim] - width, cells.shape[dim], axis=dim)
        cells = jnp.concatenate(
            [
                lax.ppermute(tail, axis, [(i, (i + 1) % count) for i in range(ends)]),
                cells,
                lax.ppermute(head, axis, [((i + 1) % count, i) for i in range(ends)]),
            ],
            axis=dim,
        )
    return cells


def hidden_state(coarse_latent, particle_type, type_table):
    picked = (particle_type[:, None] == jnp.arange(TYPES, dtype=jnp.int32)[None, :]).astype(
        jnp.bfloat16
    )
    embed = jnp.dot(picked, type_table, preferred_element_type=jnp.float32)
    return jax.nn.silu(coarse_latent.astype(jnp.float32) + embed).astype(jnp.bfloat16)


def convolve(padded, weight):
    span_p = padded.shape[0] - 2
    span_e = padded.shape[1] - 2
    summed = jnp.zeros((span_p, span_e) + padded.shape[2:], jnp.float32)
    for offset_row in range(3):
        for offset_col in range(3):
            shifted = padded[offset_row : offset_row + span_p, offset_col : offset_col + span_e]
            summed = summed + jnp.einsum(
                "pelc,cd->peld",
                shifted,
                weight[3 * offset_row + offset_col],
                preferred_element_type=jnp.float32,
            )
    return summed


def attend(query, key_rows, value_rows):
    cell_count = query.shape[0]
    width = 512
    groups = -(-cell_count // width)
    grouped = query.reshape(groups, width, HEADS, HDIM)
    keyed = key_rows.reshape(-1, HEADS, HDIM)
    valued = value_rows.reshape(-1, HEADS, HDIM)
    score_scale = 1.0 / math.sqrt(HDIM)

    def one_group(rows):
        scores = (
            jnp.einsum("bhd,thd->hbt", rows, keyed, preferred_element_type=jnp.float32)
            * score_scale
        )
        probs = jax.nn.softmax(scores, axis=-1).astype(jnp.bfloat16)
        return jnp.einsum("hbt,thd->bhd", probs, valued, preferred_element_type=jnp.float32).astype(
            jnp.bfloat16
        )

    return lax.map(one_group, grouped).reshape(groups * width, C)


def with_rims(normed):
    wrapped = padded_2(normed, (("phi", 0),), 1, True)
    return padded_2(wrapped, (("eta", 1),), 1, False)


def normalize(stream, gain):
    return (
        stream * lax.rsqrt(jnp.mean(stream * stream, axis=-1, keepdims=True) + eps) * gain
    ).astype(jnp.bfloat16)


def update(conv, normed, block_idx, coarse_kv, query_weight, mix_weight, out_weight):
    activated = jax.nn.silu(conv).astype(jnp.bfloat16)
    flat = normed.reshape(-1, C)
    query = jnp.dot(flat, query_weight[block_idx], preferred_element_type=jnp.float32).astype(
        jnp.bfloat16
    )
    start = block_idx * 2 * C
    attended = attend(
        query, coarse_kv[:, start : start + C], coarse_kv[:, start + C : start + 2 * C]
    )
    branch_one = jnp.dot(
        activated.reshape(-1, C), mix_weight[block_idx], preferred_element_type=jnp.float32
    )
    branch_two = jnp.dot(attended, out_weight[block_idx], preferred_element_type=jnp.float32)
    return (branch_one + branch_two).reshape(conv.shape)


def body(
    noisy_field,
    noise_draw,
    coarse_latent,
    particle_type,
    type_table,
    kv_weight,
    norm_gain,
    conv_weight,
    query_weight,
    mix_weight,
    out_weight,
):
    hidden = hidden_state(coarse_latent, particle_type, type_table)
    local_kv = jnp.dot(hidden, kv_weight, preferred_element_type=jnp.float32).astype(jnp.bfloat16)
    coarse_kv = lax.all_gather(local_kv, "phi", axis=0, tiled=True)
    span_p, span_e = (noisy_field.shape[0], noisy_field.shape[1])
    stream = noisy_field.astype(jnp.float32).reshape(span_p, span_e, LAYERS, C)
    for block_idx in range(BLOCKS):
        normed = normalize(stream, norm_gain[block_idx])
        padded = with_rims(normed)
        conv = convolve(padded, conv_weight[block_idx])
        stream = stream + update(
            conv, normed, block_idx, coarse_kv, query_weight, mix_weight, out_weight
        )
    flat_stream = stream.reshape(noisy_field.shape)
    denoised = 1.02 * (
        noisy_field.astype(jnp.float32) - 0.2 * flat_stream
    ) + 0.3 * noise_draw.astype(jnp.float32)
    return denoised.astype(jnp.bfloat16)


def solution(mesh):
    in_specs = (
        P("phi", "eta", None),
        P("phi", "eta", None),
        P("phi", None),
        P("phi"),
        P(),
        P(),
        P(),
        P(),
        P(),
        P(),
        P(),
    )
    out_specs = P("phi", "eta", None)
    return jax.shard_map(body, mesh=mesh, in_specs=in_specs, out_specs=out_specs, check_vma=False)
```

profile of v0, /device:TPU:8, one launch (start us, length us, event | category | flops | bytes accessed | tf_op | source)
XLA Modules:
  0.0 290.4 jit_solution(13421350984211536968)
XLA Ops:
  11.6 17.1 %collective-permute-start.1 = (bf16[1,64,8,96]{3,1,2,0:T(8,128)(2,1)}, bf16[1,64,8,96]{3,1,2,0:T(8,128)(2,1)}, u32[]{:S(2)}, u32[]{:S(2)}) collective-permute-start(bf16[1,64,8,96]{3,1,2,0:T(8,128)(2,1)} %get-tuple-element.150), channel_id=1, source_target_pairs={{4,0},{8,4},{12,8},{16,12},{20,16},{24,20},{28,24},{32,28},{36,32}... | collective-permute-start | bytes 294920 | tf_op jit(solution)/shard_map/ppermute | solution.py:29
  44.3 3.2 %collective-permute-start.3 = (bf16[6,1,8,96]{3,1,2,0:T(2,128)(2,1)S(1)}, bf16[6,1,8,96]{3,1,2,0:T(2,128)(2,1)S(1)}, u32[]{:S(2)}, u32[]{:S(2)}) collective-permute-start(bf16[6,1,8,96]{3,1,2,0:T(2,128)(2,1)S(1)} %get-tuple-element.146), channel_id=1, source_target_pairs={{1,0},{2,1},{3,2},{5,4},{6,5},{7,6},{9,8},{10,9},{11,10},{13,12},{... | collective-permute-start | bytes 27656 | tf_op jit(solution)/shard_map/ppermute | solution.py:29
  58.9 81.4 %all-gather.2.cloned.1.call-done = bf16[2048,384]{1,0:T(8,128)(2,1)} async-done(((bf16[16,384]{1,0:T(8,128)(2,1)}), bf16[2048,384]{1,0:T(8,128)(2,1)}) %all-gather.2.cloned.1.call-update) | async-done | bytes 1572880 | tf_op jit(solution)/shard_map/all_gather | solution.py:125
  140.3 3.6 %fusion.177 = (bf16[2048,96]{1,0:T(8,128)(2,1)}, bf16[2048,96]{1,0:T(8,128)(2,1)}, bf16[2048,96]{1,0:T(8,128)(2,1)S(1)}, bf16[2048,96]{1,0:T(8,128)(2,1)}) fusion(bf16[2048,384]{1,0:T(8,128)(2,1)} %all-gather.2.cloned.1.call-done), kind=kLoop, calls=%fused_computation.190 | loop fusion | bytes 3145728 | tf_op jit(solution)/shard_map/slice | solution.py:101
  146.1 47.1 %while.20 = (s32[]{:T(128)}, bf16[4,512,2,48]{1,3,2,0:T(8,128)(2,1)S(1)}, bf16[4,512,2,48]{1,3,2,0:T(8,128)(2,1)}, bf16[2048,2,48]{0,2,1:T(8,128)(2,1)S(1)}, bf16[2048,2,48]{0,2,1:T(8,128)(2,1)}, /*index=5*/s32[]{:T(128)}) while((s32[]{:T(128)}, bf16[4,512,2,48]{1,3,2,0:T(8,128)(2,1)S(1)}, bf16[4,512,2,48]{1,3,2,0:T(8,128)(2,1)}, ...), condition=%wide.region_4.5_spmd, body=%wide.region_1.4_spmd.sunk | while | flops 413190144 | bytes 19341924 | solution.py:79
  146.3 6.9 %fusion.206 = (f32[2,512]{1,0:T(2,128)S(1)}, f32[2,512,2048]{2,1,0:T(8,128)}) fusion(bf16[2048,2,48]{0,2,1:T(8,128)(2,1)S(1)} %get-tuple-element.238, bf16[4,512,2,48]{1,3,2,0:T(8,128)(2,1)} %get-tuple-element.237, s32[]{:T(128)} %get-tuple-element.229), kind=kOutput, calls=%fused_computation.188.clone.1 | convolution fusion | flops 207620096 | bytes 8884736 | tf_op jit(solution)/shard_map/while/body/eval_jaxpr/sub | solution.py:74
  153.2 4.8 %fusion.207 = bf16[4,512,2,48]{1,3,2,0:T(8,128)(2,1)S(1)} fusion(bf16[4,512,2,48]{1,3,2,0:T(8,128)(2,1)S(1)} %get-tuple-element.230, s32[]{:T(128)} %get-tuple-element.229, bf16[2048,2,48]{0,2,1:T(8,128)(2,1)S(1)} %copy-done.10, f32[2,512,2048]{2,1,0:T(8,128)} %get-tuple-element.214, f32[2,512]{1,0:T(2,128)S(1)} %get-tuple-element.215), kind=kOutput, calls=%fused_computation.9.clone.1 | convolution fusion | flops 205570048 | bytes 8884228 | tf_op jit(solution)/shard_map/while/body/eval_jaxpr/hbt,thd->bhd/dot_general | solution.py:75
  158.0 6.9 %fusion.206 = (f32[2,512]{1,0:T(2,128)S(1)}, f32[2,512,2048]{2,1,0:T(8,128)}) fusion(bf16[2048,2,48]{0,2,1:T(8,128)(2,1)S(1)} %get-tuple-element.238, bf16[4,512,2,48]{1,3,2,0:T(8,128)(2,1)} %get-tuple-element.237, s32[]{:T(128)} %get-tuple-element.229), kind=kOutput, calls=%fused_computation.188.clone.1 | convolution fusion | flops 207620096 | bytes 8884736 | tf_op jit(solution)/shard_map/while/body/eval_jaxpr/sub | solution.py:74
  164.9 4.8 %fusion.207 = bf16[4,512,2,48]{1,3,2,0:T(8,128)(2,1)S(1)} fusion(bf16[4,512,2,48]{1,3,2,0:T(8,128)(2,1)S(1)} %get-tuple-element.230, s32[]{:T(128)} %get-tuple-element.229, bf16[2048,2,48]{0,2,1:T(8,128)(2,1)S(1)} %copy-done.10, f32[2,512,2048]{2,1,0:T(8,128)} %get-tuple-element.214, f32[2,512]{1,0:T(2,128)S(1)} %get-tuple-element.215), kind=kOutput, calls=%fused_computation.9.clone.1 | convolution fusion | flops 205570048 | bytes 8884228 | tf_op jit(solution)/shard_map/while/body/eval_jaxpr/hbt,thd->bhd/dot_general | solution.py:75
  169.8 6.9 %fusion.206 = (f32[2,512]{1,0:T(2,128)S(1)}, f32[2,512,2048]{2,1,0:T(8,128)}) fusion(bf16[2048,2,48]{0,2,1:T(8,128)(2,1)S(1)} %get-tuple-element.238, bf16[4,512,2,48]{1,3,2,0:T(8,128)(2,1)} %get-tuple-element.237, s32[]{:T(128)} %get-tuple-element.229), kind=kOutput, calls=%fused_computation.188.clone.1 | convolution fusion | flops 207620096 | bytes 8884736 | tf_op jit(solution)/shard_map/while/body/eval_jaxpr/sub | solution.py:74
  176.6 4.8 %fusion.207 = bf16[4,512,2,48]{1,3,2,0:T(8,128)(2,1)S(1)} fusion(bf16[4,512,2,48]{1,3,2,0:T(8,128)(2,1)S(1)} %get-tuple-element.230, s32[]{:T(128)} %get-tuple-element.229, bf16[2048,2,48]{0,2,1:T(8,128)(2,1)S(1)} %copy-done.10, f32[2,512,2048]{2,1,0:T(8,128)} %get-tuple-element.214, f32[2,512]{1,0:T(2,128)S(1)} %get-tuple-element.215), kind=kOutput, calls=%fused_computation.9.clone.1 | convolution fusion | flops 205570048 | bytes 8884228 | tf_op jit(solution)/shard_map/while/body/eval_jaxpr/hbt,thd->bhd/dot_general | solution.py:75
  181.5 6.9 %fusion.206 = (f32[2,512]{1,0:T(2,128)S(1)}, f32[2,512,2048]{2,1,0:T(8,128)}) fusion(bf16[2048,2,48]{0,2,1:T(8,128)(2,1)S(1)} %get-tuple-element.238, bf16[4,512,2,48]{1,3,2,0:T(8,128)(2,1)} %get-tuple-element.237, s32[]{:T(128)} %get-tuple-element.229), kind=kOutput, calls=%fused_computation.188.clone.1 | convolution fusion | flops 207620096 | bytes 8884736 | tf_op jit(solution)/shard_map/while/body/eval_jaxpr/sub | solution.py:74
  188.4 4.8 %fusion.207 = bf16[4,512,2,48]{1,3,2,0:T(8,128)(2,1)S(1)} fusion(bf16[4,512,2,48]{1,3,2,0:T(8,128)(2,1)S(1)} %get-tuple-element.230, s32[]{:T(128)} %get-tuple-element.229, bf16[2048,2,48]{0,2,1:T(8,128)(2,1)S(1)} %copy-done.10, f32[2,512,2048]{2,1,0:T(8,128)} %get-tuple-element.214, f32[2,512]{1,0:T(2,128)S(1)} %get-tuple-element.215), kind=kOutput, calls=%fused_computation.9.clone.1 | convolution fusion | flops 205570048 | bytes 8884228 | tf_op jit(solution)/shard_map/while/body/eval_jaxpr/hbt,thd->bhd/dot_general | solution.py:75
  202.8 39.8 %while.21 = (s32[]{:T(128)}, bf16[4,512,2,48]{1,3,2,0:T(8,128)(2,1)S(1)}, bf16[4,512,2,48]{1,3,2,0:T(8,128)(2,1)S(1)}, bf16[2048,2,48]{0,2,1:T(8,128)(2,1)S(1)}, bf16[2048,2,48]{0,2,1:T(8,128)(2,1)S(1)}, /*index=5*/s32[]{:T(128)}) while((s32[]{:T(128)}, bf16[4,512,2,48]{1,3,2,0:T(8,128)(2,1)S(1)}, bf16[4,512,2,48]{1,3,2,0:T(8,128)(2,1)S(1)}, ...), condition=%wide.region_9.10_spmd, body=%wide.region_6.9_spmd.sunk | while | flops 413190144 | bytes 17768524 | solution.py:79
  202.8 5.1 %fusion.211 = (f32[2,512]{1,0:T(2,128)S(1)}, f32[2,512,2048]{2,1,0:T(8,128)}) fusion(bf16[2048,2,48]{0,2,1:T(8,128)(2,1)S(1)} %get-tuple-element.256, bf16[4,512,2,48]{1,3,2,0:T(8,128)(2,1)S(1)} %get-tuple-element.255, s32[]{:T(128)} %get-tuple-element.247), kind=kOutput, calls=%fused_computation.189.clone.1 | convolution fusion | flops 207620096 | bytes 8884228 | tf_op jit(solution)/shard_map/while/body/eval_jaxpr/sub | solution.py:74
  207.9 4.8 %fusion.212 = bf16[4,512,2,48]{1,3,2,0:T(8,128)(2,1)S(1)} fusion(bf16[4,512,2,48]{1,3,2,0:T(8,128)(2,1)S(1)} %get-tuple-element.248, s32[]{:T(128)} %get-tuple-element.247, bf16[2048,2,48]{0,2,1:T(8,128)(2,1)S(1)} %get-tuple-element.257, f32[2,512,2048]{2,1,0:T(8,128)} %get-tuple-element.221, f32[2,512]{1,0:T(2,128)S(1)} %get-tuple-element.222), kind=kOutput, calls=%fused_computation.28.clone.1 | convolution fusion | flops 205570048 | bytes 8884228 | tf_op jit(solution)/shard_map/while/body/eval_jaxpr/hbt,thd->bhd/dot_general | solution.py:75
  212.7 5.1 %fusion.211 = (f32[2,512]{1,0:T(2,128)S(1)}, f32[2,512,2048]{2,1,0:T(8,128)}) fusion(bf16[2048,2,48]{0,2,1:T(8,128)(2,1)S(1)} %get-tuple-element.256, bf16[4,512,2,48]{1,3,2,0:T(8,128)(2,1)S(1)} %get-tuple-element.255, s32[]{:T(128)} %get-tuple-element.247), kind=kOutput, calls=%fused_computation.189.clone.1 | convolution fusion | flops 207620096 | bytes 8884228 | tf_op jit(solution)/shard_map/while/body/eval_jaxpr/sub | solution.py:74
  217.8 4.8 %fusion.212 = bf16[4,512,2,48]{1,3,2,0:T(8,128)(2,1)S(1)} fusion(bf16[4,512,2,48]{1,3,2,0:T(8,128)(2,1)S(1)} %get-tuple-element.248, s32[]{:T(128)} %get-tuple-element.247, bf16[2048,2,48]{0,2,1:T(8,128)(2,1)S(1)} %get-tuple-element.257, f32[2,512,2048]{2,1,0:T(8,128)} %get-tuple-element.221, f32[2,512]{1,0:T(2,128)S(1)} %get-tuple-element.222), kind=kOutput, calls=%fused_computation.28.clone.1 | convolution fusion | flops 205570048 | bytes 8884228 | tf_op jit(solution)/shard_map/while/body/eval_jaxpr/hbt,thd->bhd/dot_general | solution.py:75
  222.7 5.1 %fusion.211 = (f32[2,512]{1,0:T(2,128)S(1)}, f32[2,512,2048]{2,1,0:T(8,128)}) fusion(bf16[2048,2,48]{0,2,1:T(8,128)(2,1)S(1)} %get-tuple-element.256, bf16[4,512,2,48]{1,3,2,0:T(8,128)(2,1)S(1)} %get-tuple-element.255, s32[]{:T(128)} %get-tuple-element.247), kind=kOutput, calls=%fused_computation.189.clone.1 | convolution fusion | flops 207620096 | bytes 8884228 | tf_op jit(solution)/shard_map/while/body/eval_jaxpr/sub | solution.py:74
  227.8 4.8 %fusion.212 = bf16[4,512,2,48]{1,3,2,0:T(8,128)(2,1)S(1)} fusion(bf16[4,512,2,48]{1,3,2,0:T(8,128)(2,1)S(1)} %get-tuple-element.248, s32[]{:T(128)} %get-tuple-element.247, bf16[2048,2,48]{0,2,1:T(8,128)(2,1)S(1)} %get-tuple-element.257, f32[2,512,2048]{2,1,0:T(8,128)} %get-tuple-element.221, f32[2,512]{1,0:T(2,128)S(1)} %get-tuple-element.222), kind=kOutput, calls=%fused_computation.28.clone.1 | convolution fusion | flops 205570048 | bytes 8884228 | tf_op jit(solution)/shard_map/while/body/eval_jaxpr/hbt,thd->bhd/dot_general | solution.py:75
  232.6 5.1 %fusion.211 = (f32[2,512]{1,0:T(2,128)S(1)}, f32[2,512,2048]{2,1,0:T(8,128)}) fusion(bf16[2048,2,48]{0,2,1:T(8,128)(2,1)S(1)} %get-tuple-element.256, bf16[4,512,2,48]{1,3,2,0:T(8,128)(2,1)S(1)} %get-tuple-element.255, s32[]{:T(128)} %get-tuple-element.247), kind=kOutput, calls=%fused_computation.189.clone.1 | convolution fusion | flops 207620096 | bytes 8884228 | tf_op jit(solution)/shard_map/while/body/eval_jaxpr/sub | solution.py:74
  237.7 4.8 %fusion.212 = bf16[4,512,2,48]{1,3,2,0:T(8,128)(2,1)S(1)} fusion(bf16[4,512,2,48]{1,3,2,0:T(8,128)(2,1)S(1)} %get-tuple-element.248, s32[]{:T(128)} %get-tuple-element.247, bf16[2048,2,48]{0,2,1:T(8,128)(2,1)S(1)} %get-tuple-element.257, f32[2,512,2048]{2,1,0:T(8,128)} %get-tuple-element.221, f32[2,512]{1,0:T(2,128)S(1)} %get-tuple-element.222), kind=kOutput, calls=%fused_computation.28.clone.1 | convolution fusion | flops 205570048 | bytes 8884228 | tf_op jit(solution)/shard_map/while/body/eval_jaxpr/hbt,thd->bhd/dot_general | solution.py:75
  249.0 11.5 %collective-permute-start.5 = (bf16[1,64,8,96]{3,1,2,0:T(8,128)(2,1)S(1)}, bf16[1,64,8,96]{3,1,2,0:T(8,128)(2,1)S(1)}, u32[]{:S(2)}, u32[]{:S(2)}) collective-permute-start(bf16[1,64,8,96]{3,1,2,0:T(8,128)(2,1)S(1)} %copy-done.11), channel_id=1, source_target_pairs={{4,0},{8,4},{12,8},{16,12},{20,16},{24,20},{28,24},{32,28},{36,32}... | collective-permute-start | bytes 294920 | tf_op jit(solution)/shard_map/ppermute | solution.py:29
  266.4 4.1 %collective-permute-start.7 = (bf16[6,1,8,96]{3,1,2,0:T(2,128)(2,1)S(1)}, bf16[6,1,8,96]{3,1,2,0:T(2,128)(2,1)S(1)}, u32[]{:S(2)}, u32[]{:S(2)}) collective-permute-start(bf16[6,1,8,96]{3,1,2,0:T(2,128)(2,1)S(1)} %get-tuple-element.142), channel_id=1, source_target_pairs={{1,0},{2,1},{3,2},{5,4},{6,5},{7,6},{9,8},{10,9},{11,10},{13,12},{... | collective-permute-start | bytes 27656 | tf_op jit(solution)/shard_map/ppermute | solution.py:29
  (143 shorter events, 68.5 us)
Async XLA Ops:
  6.5 22.2 %copy-start = (bf16[512,384]{1,0:T(8,128)(2,1)S(1)}, bf16[512,384]{1,0:T(8,128)(2,1)}, u32[]{:S(2)}) copy-start(bf16[512,384]{1,0:T(8,128)(2,1)} %param.20) | copy-start | bytes 1179652
  6.5 133.8 %all-gather.2.cloned.1.call-start = ((), (), s32[]{:S(2)}) async-start(), calls=%async_computation | async-start | bytes 1585152 | tf_op jit(solution)/shard_map/all_gather | solution.py:125
  8.1 20.6 %copy-start.18 = (bf16[16,512]{1,0:T(8,128)(2,1)S(1)}, bf16[16,512]{1,0:T(8,128)(2,1)}, u32[]{:S(2)}) copy-start(bf16[16,512]{1,0:T(8,128)(2,1)} %param.17) | copy-start | bytes 49156
  8.1 20.6 %copy-start.19 = (bf16[8,512]{1,0:T(8,128)(2,1)S(1)}, bf16[8,512]{1,0:T(8,128)(2,1)}, u32[]{:S(2)}) copy-start(bf16[8,512]{1,0:T(8,128)(2,1)} %param.19) | copy-start | bytes 24580
  8.1 20.6 %copy-start.21 = (s32[16]{0:T(128)S(1)}, s32[16]{0:T(128)}, u32[]{:S(2)}) copy-start(s32[16]{0:T(128)} %param.18) | copy-start | bytes 196
  9.7 31.3 %collective-permute-start = (bf16[1,64,8,96]{3,1,2,0:T(8,128)(2,1)}, bf16[1,64,8,96]{3,1,2,0:T(8,128)(2,1)S(1)}, u32[]{:S(2)}, u32[]{:S(2)}) collective-permute-start(bf16[1,64,8,96]{3,1,2,0:T(8,128)(2,1)} %get-tuple-element.149), channel_id=1, source_target_pairs={{0,4},{4,8},{8,12},{12,16},{16,20},{20,24},{24,28},{28,32},{32,36}... | collective-permute-start | bytes 294920 | tf_op jit(solution)/shard_map/ppermute | solution.py:27
  11.6 19.9 %copy-start.2 = (bf16[4,64,768]{2,1,0:T(8,128)(2,1)S(1)}, bf16[4,64,768]{2,1,0:T(8,128)(2,1)}, u32[]{:S(2)}) copy-start(bf16[4,64,768]{2,1,0:T(8,128)(2,1)} %param.15) | copy-start | bytes 1179652
  11.6 29.3 %collective-permute-start.1 = (bf16[1,64,8,96]{3,1,2,0:T(8,128)(2,1)}, bf16[1,64,8,96]{3,1,2,0:T(8,128)(2,1)}, u32[]{:S(2)}, u32[]{:S(2)}) collective-permute-start(bf16[1,64,8,96]{3,1,2,0:T(8,128)(2,1)} %get-tuple-element.150), channel_id=1, source_target_pairs={{4,0},{8,4},{12,8},{16,12},{20,16},{24,20},{28,24},{32,28},{36,32}... | collective-permute-start | bytes 294920 | tf_op jit(solution)/shard_map/ppermute | solution.py:29
  41.7 8.1 %collective-permute-start.2 = (bf16[6,1,8,96]{3,1,2,0:T(2,128)(2,1)S(1)}, bf16[6,1,8,96]{3,1,2,0:T(2,128)(2,1)S(1)}, u32[]{:S(2)}, u32[]{:S(2)}) collective-permute-start(bf16[6,1,8,96]{3,1,2,0:T(2,128)(2,1)S(1)} %get-tuple-element.145), channel_id=1, source_target_pairs={{0,1},{1,2},{2,3},{4,5},{5,6},{6,7},{8,9},{9,10},{10,11},{12,13},{... | collective-permute-start | bytes 27656 | tf_op jit(solution)/shard_map/ppermute | solution.py:27
  44.3 5.7 %collective-permute-start.3 = (bf16[6,1,8,96]{3,1,2,0:T(2,128)(2,1)S(1)}, bf16[6,1,8,96]{3,1,2,0:T(2,128)(2,1)S(1)}, u32[]{:S(2)}, u32[]{:S(2)}) collective-permute-start(bf16[6,1,8,96]{3,1,2,0:T(2,128)(2,1)S(1)} %get-tuple-element.146), channel_id=1, source_target_pairs={{1,0},{2,1},{3,2},{5,4},{6,5},{7,6},{9,8},{10,9},{11,10},{13,12},{... | collective-permute-start | bytes 27656 | tf_op jit(solution)/shard_map/ppermute | solution.py:29
  146.1 47.5 %copy-start.12 = (bf16[2,96,96]{2,1,0:T(8,128)(2,1)S(1)}, bf16[2,96,96]{2,1,0:T(8,128)(2,1)}, u32[]{:S(2)}) copy-start(bf16[2,96,96]{2,1,0:T(8,128)(2,1)} %param.25) | copy-start | bytes 110596
  146.3 6.9 %copy-start.10 = (bf16[2048,2,48]{0,2,1:T(8,128)(2,1)S(1)}, bf16[2048,2,48]{0,2,1:T(8,128)(2,1)}, u32[]{:S(2)}) copy-start(bf16[2048,2,48]{0,2,1:T(8,128)(2,1)} %get-tuple-element.239) | copy-start | bytes 1179652 | tf_op jit(solution)/shard_map/while
  158.0 6.9 %copy-start.10 = (bf16[2048,2,48]{0,2,1:T(8,128)(2,1)S(1)}, bf16[2048,2,48]{0,2,1:T(8,128)(2,1)}, u32[]{:S(2)}) copy-start(bf16[2048,2,48]{0,2,1:T(8,128)(2,1)} %get-tuple-element.239) | copy-start | bytes 1179652 | tf_op jit(solution)/shard_map/while
  169.8 6.9 %copy-start.10 = (bf16[2048,2,48]{0,2,1:T(8,128)(2,1)S(1)}, bf16[2048,2,48]{0,2,1:T(8,128)(2,1)}, u32[]{:S(2)}) copy-start(bf16[2048,2,48]{0,2,1:T(8,128)(2,1)} %get-tuple-element.239) | copy-start | bytes 1179652 | tf_op jit(solution)/shard_map/while
  181.5 6.9 %copy-start.10 = (bf16[2048,2,48]{0,2,1:T(8,128)(2,1)S(1)}, bf16[2048,2,48]{0,2,1:T(8,128)(2,1)}, u32[]{:S(2)}) copy-start(bf16[2048,2,48]{0,2,1:T(8,128)(2,1)} %get-tuple-element.239) | copy-start | bytes 1179652 | tf_op jit(solution)/shard_map/while
  198.6 3.7 %copy-start.7 = (bf16[2048,96]{1,0:T(8,128)(2,1)S(1)}, bf16[2048,96]{1,0:T(8,128)(2,1)}, u32[]{:S(2)}) copy-start(bf16[2048,96]{1,0:T(8,128)(2,1)} %get-tuple-element.136) | copy-start | bytes 1179652
  198.6 3.9 %copy-start.6 = (bf16[2048,96]{1,0:T(8,128)(2,1)S(1)}, bf16[2048,96]{1,0:T(8,128)(2,1)}, u32[]{:S(2)}) copy-start(bf16[2048,96]{1,0:T(8,128)(2,1)} %get-tuple-element.135) | copy-start | bytes 1179652
  242.6 3.2 %copy-start.8 = (bf16[4,512,2,48]{1,3,2,0:T(8,128)(2,1)}, bf16[4,512,2,48]{1,3,2,0:T(8,128)(2,1)S(1)}, u32[]{:S(2)}) copy-start(bf16[4,512,2,48]{1,3,2,0:T(8,128)(2,1)S(1)} %get-tuple-element.60) | copy-start | bytes 1179652
  242.6 4.5 %copy-start.4 = (f32[4,64,768]{2,1,0:T(8,128)S(1)}, f32[4,64,768]{2,1,0:T(8,128)}, u32[]{:S(2)}) copy-start(f32[4,64,768]{2,1,0:T(8,128)} %reshape.137) | copy-start | bytes 2359300
  243.3 18.6 %collective-permute-start.4 = (bf16[1,64,8,96]{3,1,2,0:T(8,128)(2,1)}, bf16[1,64,8,96]{3,1,2,0:T(8,128)(2,1)S(1)}, u32[]{:S(2)}, u32[]{:S(2)}) collective-permute-start(bf16[1,64,8,96]{3,1,2,0:T(8,128)(2,1)} %get-tuple-element.147), channel_id=1, source_target_pairs={{0,4},{4,8},{8,12},{12,16},{16,20},{20,24},{24,28},{28,32},{32,36}... | collective-permute-start | bytes 294920 | tf_op jit(solution)/shard_map/ppermute | solution.py:27
  248.4 13.1 %copy-start.9 = (bf16[4,512,2,48]{1,3,2,0:T(8,128)(2,1)S(1)}, bf16[4,512,2,48]{1,3,2,0:T(8,128)(2,1)}, u32[]{:S(2)}) copy-start(bf16[4,512,2,48]{1,3,2,0:T(8,128)(2,1)} %copy-done.8) | copy-start | bytes 1179652
  249.0 15.5 %collective-permute-start.5 = (bf16[1,64,8,96]{3,1,2,0:T(8,128)(2,1)S(1)}, bf16[1,64,8,96]{3,1,2,0:T(8,128)(2,1)S(1)}, u32[]{:S(2)}, u32[]{:S(2)}) collective-permute-start(bf16[1,64,8,96]{3,1,2,0:T(8,128)(2,1)S(1)} %copy-done.11), channel_id=1, source_target_pairs={{4,0},{8,4},{12,8},{16,12},{20,16},{24,20},{28,24},{32,28},{36,32}... | collective-permute-start | bytes 294920 | tf_op jit(solution)/shard_map/ppermute | solution.py:29
  264.5 8.1 %collective-permute-start.6 = (bf16[6,1,8,96]{3,1,2,0:T(2,128)(2,1)S(1)}, bf16[6,1,8,96]{3,1,2,0:T(2,128)(2,1)S(1)}, u32[]{:S(2)}, u32[]{:S(2)}) collective-permute-start(bf16[6,1,8,96]{3,1,2,0:T(2,128)(2,1)S(1)} %get-tuple-element.141), channel_id=1, source_target_pairs={{0,1},{1,2},{2,3},{4,5},{5,6},{6,7},{8,9},{9,10},{10,11},{12,13},{... | collective-permute-start | bytes 27656 | tf_op jit(solution)/shard_map/ppermute | solution.py:27
  266.4 6.2 %collective-permute-start.7 = (bf16[6,1,8,96]{3,1,2,0:T(2,128)(2,1)S(1)}, bf16[6,1,8,96]{3,1,2,0:T(2,128)(2,1)S(1)}, u32[]{:S(2)}, u32[]{:S(2)}) collective-permute-start(bf16[6,1,8,96]{3,1,2,0:T(2,128)(2,1)S(1)} %get-tuple-element.142), channel_id=1, source_target_pairs={{1,0},{2,1},{3,2},{5,4},{6,5},{7,6},{9,8},{10,9},{11,10},{13,12},{... | collective-permute-start | bytes 27656 | tf_op jit(solution)/shard_map/ppermute | solution.py:29
  (10 other events, 18.9 us)
Sparse Core Ops, SparseCore 0:
  29.8 110.4 all-gather.1
where the time goes:
time: 293 us; the launch traced here: 290 us
  matrix products  113 us (39%)
  waiting for transfers between devices  84.1 us (29%)
  starting transfers between devices  44.6 us (15%)
  local copies, waits for them, and re-layouts  25.6 us (9%)
  between operations  14.1 us (5%)
  other arithmetic  8.84 us (3%)
    all_gather x1, waiting for transfers between devices, body(): coarse_kv = lax.all_gather(local_kv, 'phi', axis=0, tiled=True)  81.4 us
    sub x8, matrix products, one_group(): probs = jax.nn.softmax(scores, axis=-1).astype(jnp.bfloat16)  47.8 us
    dot_general x8, matrix products, one_group(): jnp.einsum('hbt,thd->bhd', probs, valued, preferred_element_type=jnp.floa...  38.6 us
    ppermute x4, starting transfers between devices, padded_2(): lax.ppermute(head, axis, [((i + 1) % count, i) for i in range(ends)])  36 us
    dot_general x18, matrix products, convolve(): jnp.einsum('pelc,cd->peld', shifted, weight[3 * offset_row + offset_col],...  20.5 us
    ppermute x4, starting transfers between devices, padded_2(): lax.ppermute(tail, axis, [(i, (i + 1) % count) for i in range(ends)])  8.58 us
  transfers between devices with their start and end apart: 9, of which 3 were waited for; matrix products, arithmetic and copies ran while one was open for 11% of the time, Pallas kernels for 0%

commit v1 on v0

v1 whole, which is shorter than its diff:
```python
import math

import jax
import jax.numpy as jnp
from jax import lax
from jax.experimental import pallas as pl
from jax.experimental.pallas import tpu as pltpu
from jax.sharding import PartitionSpec as P

C = 96
LATENT = 512
TYPES = 8
HEADS = 2
BLOCKS = 2
LAYERS = 8
HDIM = 48
LANES = 128
EPS = 1e-06
SCORE_SCALE = 1.0 / math.sqrt(HDIM) * math.log2(math.e)
SAFE_SCORE = 96.0

F32 = jnp.float32
BF16 = jnp.bfloat16


def dot(a, b):
    return jnp.dot(a, b, preferred_element_type=F32)


def silu(x):
    return x / (1.0 + jnp.exp(-x))


def tokens_kernel(type_ref, latent_ref, table_ref, weight_ref, kv_ref):
    rows = latent_ref.shape[0]
    row = lax.broadcasted_iota(jnp.int32, (rows, TYPES), 0)
    column = lax.broadcasted_iota(jnp.int32, (rows, TYPES), 1)
    kind = jnp.zeros((rows, TYPES), jnp.int32)
    for i in range(rows):
        kind = jnp.where(row == i, type_ref[i], kind)
    picked = (kind == column).astype(F32).astype(BF16)
    embed = dot(picked, table_ref[...])
    hidden = jax.nn.silu(latent_ref[...].astype(F32) + embed).astype(BF16)
    kv_ref[...] = dot(hidden, weight_ref[...]).astype(BF16)


def local_tokens(coarse_latent, particle_type, type_table, kv_weight):
    vmem = pl.BlockSpec(memory_space=pltpu.VMEM)
    return pl.pallas_call(
        tokens_kernel,
        out_shape=jax.ShapeDtypeStruct((coarse_latent.shape[0], kv_weight.shape[1]), BF16),
        in_specs=[pl.BlockSpec(memory_space=pltpu.SMEM), vmem, vmem, vmem],
        out_specs=vmem,
        cost_estimate=pl.CostEstimate(flops=6_000_000, bytes_accessed=500_000, transcendentals=8192),
        name="tokens",
    )(particle_type, coarse_latent, type_table, kv_weight)


def phi_index(x, y, z, core):
    return ((x * 2 + y) * 8 + z) * 2 + core


YZ_GROUPS = [
    [phi_index(x, y, z, c) for y in range(2) for z in range(8)] for x in range(4) for c in range(2)
]
X_GROUPS = [
    [phi_index(x, y, z, c) for x in range(4)] for y in range(2) for z in range(8) for c in range(2)
]


def spread(rows, groups):
    count = len(groups[0])
    copies = jnp.broadcast_to(rows[None], (count,) + rows.shape)
    return lax.all_to_all(
        copies, "phi", 0, 0, tiled=True, axis_index_groups=groups
    ).reshape(-1, rows.shape[-1])


def gather_tokens(kv):
    count = lax.axis_size("phi")
    if count != 128:
        return lax.all_gather(kv, "phi", axis=0, tiled=True)
    kv = spread(kv, YZ_GROUPS)
    kv = spread(kv, X_GROUPS)
    other = lax.ppermute(kv, "phi", [(i, i ^ 1) for i in range(count)])
    return jnp.concatenate([kv, other], axis=0)


def halo(field):
    count = lax.axis_size("phi")
    up = [(i, (i + 1) % count) for i in range(count)]
    down = [((i + 1) % count, i) for i in range(count)]
    top = lax.ppermute(field[-2:], "phi", up)
    bottom = lax.ppermute(field[:2], "phi", down)
    bands = lax.axis_size("eta")
    right = [(i, i + 1) for i in range(bands - 1)]
    left = [(i + 1, i) for i in range(bands - 1)]
    west = jnp.concatenate([top[:, -2:], field[:, -2:], bottom[:, -2:]], axis=0)
    east = jnp.concatenate([top[:, :2], field[:, :2], bottom[:, :2]], axis=0)
    return top, bottom, lax.ppermute(west, "eta", right), lax.ppermute(east, "eta", left)


def normalized(x, gain):
    mean = jnp.sum(x * x, axis=-1, keepdims=True) * (1.0 / C)
    return (x * lax.rsqrt(mean + EPS) * gain).astype(BF16)


def conv_branch(taps, row, start, length, weight_ref, mix_ref):
    conv = jnp.zeros((length, C), F32)
    for di in range(3):
        for dj in range(3):
            shifted = taps[row + di, start + 8 * dj : start + 8 * dj + length, :]
            conv = conv + dot(shifted, weight_ref[3 * di + dj])
    return dot(silu(conv).astype(BF16), mix_ref[...])


def front_kernel(
    field_ref, top_ref, bottom_ref, west_ref, east_ref, gain_ref, conv_ref, query_ref, mix_ref,
    acc_ref, q_ref, cells, taps,
):
    span_p, span_e = field_ref.shape[0], field_ref.shape[1]

    def put(row, start, piece):
        count = piece.shape[0]
        zeros = jnp.zeros((count, LANES - C), F32)
        for layer in range(LAYERS):
            part = piece[:, layer * C : (layer + 1) * C]
            cells[row, pl.ds(start * LAYERS + layer, count, stride=LAYERS), :] = jnp.concatenate(
                [part, zeros], axis=1
            )

    for row in range(span_p + 4):
        if row < 2:
            middle = top_ref[row]
        elif row < span_p + 2:
            middle = field_ref[row - 2]
        else:
            middle = bottom_ref[row - span_p - 2]
        put(row, 2, middle.astype(F32))
        put(row, 0, west_ref[row].astype(F32))
        put(row, span_e + 2, east_ref[row].astype(F32))
    for row in range(span_p + 4):
        taps[row] = normalized(cells[row][:, :C], gain_ref[...])
    length = (span_e + 2) * LAYERS
    for row in range(span_p + 2):
        branch = conv_branch(taps, row, 0, length, conv_ref, mix_ref)
        acc_ref[row] = cells[row + 1, 8 : 8 + length, :C] + branch
        q = dot(taps[row + 1, 8 : 8 + length, :], query_ref[...]) * SCORE_SCALE
        q_ref[row] = q.astype(BF16)


def front(field, top, bottom, west, east, gain, conv_weight, query_weight, mix_weight):
    span_p, span_e = field.shape[0], field.shape[1]
    vmem = pl.BlockSpec(memory_space=pltpu.VMEM)
    rows, width = span_p + 2, (span_e + 2) * LAYERS
    return pl.pallas_call(
        front_kernel,
        out_shape=[
            jax.ShapeDtypeStruct((rows, width, C), F32),
            jax.ShapeDtypeStruct((rows, width, C), BF16),
        ],
        in_specs=[vmem] * 9,
        out_specs=[vmem] * 2,
        scratch_shapes=[
            pltpu.VMEM((span_p + 4, (span_e + 4) * LAYERS, LANES), F32),
            pltpu.VMEM((span_p + 4, (span_e + 4) * LAYERS, C), BF16),
        ],
        compiler_params=pltpu.CompilerParams(vmem_limit_bytes=40 * 1024 * 1024),
        cost_estimate=pl.CostEstimate(flops=6_000_000_000, bytes_accessed=5_000_000, transcendentals=400_000),
        name="front",
    )(field, top, bottom, west, east, gain, conv_weight, query_weight, mix_weight)


def prepare_tokens(kv_ref, block, keys, values):
    start = 2 * C * block
    keys[block] = jnp.transpose(kv_ref[:, start : start + C])
    value = kv_ref[:, start + C : start + 2 * C]
    value = jnp.concatenate([value, jnp.zeros((value.shape[0], LANES - C), BF16)], axis=1)
    lane = lax.broadcasted_iota(jnp.int32, value.shape, 1)
    for head in range(HEADS):
        mine = (lane >= head * HDIM) & (lane < (head + 1) * HDIM)
        one = (lane == C).astype(BF16)
        values[block, head] = jnp.where(mine, value, one)


def largest_key(keys, block, head):
    key = keys[block, head * HDIM : (head + 1) * HDIM, :].astype(F32)
    return jnp.max(jnp.sum(key * key, axis=0, keepdims=True))


def attend(q, block, keys, values, safe):
    result = None
    lane = lax.broadcasted_iota(jnp.int32, (q.shape[0], C), 1)
    for head in range(HEADS):
        span = slice(head * HDIM, (head + 1) * HDIM)
        scores = dot(q[:, span], keys[block, span, :])
        if not safe:
            scores = scores - jnp.max(scores, axis=-1, keepdims=True)
        probs = jnp.exp2(scores).astype(BF16)
        out = dot(probs, values[block, head])
        out = out[:, :C] * (1.0 / out[:, C : C + 1])
        result = out if head == 0 else jnp.where(lane < HDIM, result, out)
    return result.astype(BF16)


def within(q, biggest):
    q = q.astype(F32)
    square = q * q
    lane = lax.broadcasted_iota(jnp.int32, q.shape, 1)
    first = jnp.sum(jnp.where(lane < HDIM, square, 0.0), axis=-1, keepdims=True)
    second = jnp.sum(jnp.where(lane < HDIM, 0.0, square), axis=-1, keepdims=True)
    worst = jnp.maximum(jnp.max(first) * biggest[0], jnp.max(second) * biggest[1])
    return worst <= SAFE_SCORE * SAFE_SCORE


def back_kernel(
    edge_ref, acc_ref, q_ref, kv_ref, field_ref, noise_ref, gain_ref, conv_ref, query_ref, mix_ref,
    out_ref, result_ref, keys, values, attended, stream, taps, flat,
):
    span_p, span_e = field_ref.shape[0], field_ref.shape[1]
    width, inner = (span_e + 2) * LAYERS, span_e * LAYERS
    for block in range(BLOCKS):
        prepare_tokens(kv_ref, block, keys, values)
    biggest = [[largest_key(keys, b, h) for h in range(HEADS)] for b in range(BLOCKS)]

    def attend_rows(q, block, rows):
        fine = within(q, biggest[block])

        @pl.when(fine)
        def _():
            attended[0:rows, :] = attend(q, block, keys, values, True)

        @pl.when(jnp.logical_not(fine))
        def _():
            attended[0:rows, :] = attend(q, block, keys, values, False)

    @pl.loop(0, span_p + 2)
    def _(row):
        attend_rows(q_ref[row], 0, width)
        new = acc_ref[row] + dot(attended[...], out_ref[0])
        stream[row] = new
        place = lax.broadcasted_iota(jnp.int32, new.shape, 0)
        outside = ((place < LAYERS) & (edge_ref[0] == 1)) | (
            (place >= width - LAYERS) & (edge_ref[1] == 1)
        )
        taps[row] = normalized(jnp.where(outside, 0.0, new), gain_ref[...])

    @pl.loop(0, span_p)
    def _(row):
        branch = conv_branch(taps, row, 0, inner, conv_ref, mix_ref)
        q = dot(taps[row + 1, LAYERS : LAYERS + inner, :], query_ref[...]) * SCORE_SCALE
        attend_rows(q.astype(BF16), 1, inner)
        new = stream[row + 1, LAYERS : LAYERS + inner, :] + branch
        new = new + dot(attended[0:inner, :], out_ref[1])
        flat[...] = jnp.concatenate([new, jnp.zeros((inner, LANES - C), F32)], axis=1)
        for layer in range(LAYERS):
            last = flat[pl.ds(layer, span_e, stride=LAYERS), :][:, :C]
            span = slice(layer * C, (layer + 1) * C)
            field = field_ref[row, :, span].astype(F32)
            noise = noise_ref[row, :, span].astype(F32)
            result_ref[row, :, span] = (1.02 * (field - 0.2 * last) + 0.3 * noise).astype(BF16)


def back(edges, acc, q, kv, field, noise, gain, conv_weight, query_weight, mix_weight, out_weight):
    span_p, span_e = field.shape[0], field.shape[1]
    vmem = pl.BlockSpec(memory_space=pltpu.VMEM)
    tokens = kv.shape[0]
    rows, width = span_p + 2, (span_e + 2) * LAYERS
    return pl.pallas_call(
        back_kernel,
        out_shape=jax.ShapeDtypeStruct(field.shape, BF16),
        in_specs=[pl.BlockSpec(memory_space=pltpu.SMEM)] + [vmem] * 10,
        out_specs=vmem,
        scratch_shapes=[
            pltpu.VMEM((BLOCKS, C, tokens), BF16),
            pltpu.VMEM((BLOCKS, HEADS, tokens, LANES), BF16),
            pltpu.VMEM((width, C), BF16),
            pltpu.VMEM((rows, width, C), F32),
            pltpu.VMEM((rows, width, C), BF16),
            pltpu.VMEM((span_e * LAYERS, LANES), F32),
        ],
        compiler_params=pltpu.CompilerParams(vmem_limit_bytes=52 * 1024 * 1024),
        cost_estimate=pl.CostEstimate(
            flops=20_000_000_000, bytes_accessed=6_000_000, transcendentals=21_000_000
        ),
        name="back",
    )(edges, acc, q, kv, field, noise, gain, conv_weight, query_weight, mix_weight, out_weight)


def body(
    noisy_field,
    noise_draw,
    coarse_latent,
    particle_type,
    type_table,
    kv_weight,
    norm_gain,
    conv_weight,
    query_weight,
    mix_weight,
    out_weight,
):
    top, bottom, west, east = halo(noisy_field)
    local = local_tokens(coarse_latent, particle_type, type_table, kv_weight)
    kv = gather_tokens(local)
    acc, q = front(
        noisy_field, top, bottom, west, east, norm_gain[0:1], conv_weight[0], query_weight[0],
        mix_weight[0],
    )
    band = lax.axis_index("eta")
    edges = jnp.stack([band == 0, band == lax.axis_size("eta") - 1]).astype(jnp.int32)
    return back(
        edges, acc, q, kv, noisy_field, noise_draw, norm_gain[1:2], conv_weight[1],
        query_weight[1], mix_weight[1], out_weight,
    )


def solution(mesh):
    in_specs = (
        P("phi", "eta", None),
        P("phi", "eta", None),
        P("phi", None),
        P("phi"),
        P(),
        P(),
        P(),
        P(),
        P(),
        P(),
        P(),
    )
    out_specs = P("phi", "eta", None)
    return jax.shard_map(body, mesh=mesh, in_specs=in_specs, out_specs=out_specs, check_vma=False)
```

time: 293 us -> 112 us (0.38)
  the two profiles are of different devices: /device:TPU:8 before, /device:TPU:1 now
where the time goes in v1:
time: 112 us; the launch traced here: 111 us
  Pallas kernels  51.1 us (46%)
  starting transfers between devices  37.6 us (34%)
  waiting for transfers between devices  15.9 us (14%)
  local copies, waits for them, and re-layouts  4.71 us (4%)
  other arithmetic  1.47 us (1%)
    pallas_call x1, Pallas kernels, back(): pl.pallas_call(back_kernel, out_shape=jax.ShapeDtypeStruct(field.shape, B...  39.3 us
    all_to_all x2, starting transfers between devices, spread(): lax.all_to_all(copies, 'phi', 0, 0, tiled=True, axis_index_groups=groups)  20.2 us
    all_to_all x2, waiting for transfers between devices, spread(): lax.all_to_all(copies, 'phi', 0, 0, tiled=True, axis_index_groups=groups)  11.4 us
    pallas_call x1, Pallas kernels, front(): pl.pallas_call(front_kernel, out_shape=[jax.ShapeDtypeStruct((rows, width...  9.79 us
    ppermute x1, starting transfers between devices, gather_tokens(): other = lax.ppermute(kv, 'phi', [(i, i ^ 1) for i in range(count)])  5.42 us
    ppermute x1, waiting for transfers between devices, halo(): lax.ppermute(east, 'eta', left)  4.56 us
    ppermute x1, starting transfers between devices, halo(): lax.ppermute(west, 'eta', right)  4.37 us
    ppermute x1, starting transfers between devices, halo(): top = lax.ppermute(field[-2:], 'phi', up)  3.45 us
  transfers between devices with their start and end apart: 7, of which 3 were waited for; matrix products, arithmetic and copies ran while one was open for 2% of the time, Pallas kernels for 9%

profile of v1, /device:TPU:1, one launch (start us, length us, event | category | flops | bytes accessed | tf_op | source)
XLA Modules:
  0.0 111.1 jit_solution(7754605658203030449)
XLA Ops:
  0.0 2.0 %tokens.1 = bf16[16,384]{1,0:T(8,128)(2,1)} custom-call(s32[16]{0:T(128)} %type_ref.1, bf16[16,512]{1,0:T(8,128)(2,1)} %latent_ref.1, bf16[8,512]{1,0:T(8,128)(2,1)} %table_ref.1, bf16[512,384]{1,0:T(8,128)(2,1)} %weight_ref.1), custom_call_target="tpu_custom_call" | custom-call | flops 6000000 | bytes 500000 | tf_op jit(solution)/shard_map/tokens/pallas_call | solution.py:49
  2.0 1.4 %broadcast_in_dim.6 = bf16[16,16,384]{2,1,0:T(8,128)(2,1)} broadcast(bf16[16,384]{1,0:T(8,128)(2,1)} %tokens.1), dimensions={1,2} | broadcast | bytes 208896 | tf_op jit(solution)/shard_map/broadcast_in_dim | solution.py:73
  3.4 16.2 %all-to-all-start = ((bf16[16,16,384]{2,1,0:T(8,128)(2,1)}), bf16[16,16,384]{2,1,0:T(8,128)(2,1)S(1)}, u32[]{:S(2)}, u32[]{:S(2)}) async-start(bf16[16,16,384]{2,1,0:T(8,128)(2,1)} %broadcast_in_dim.6), calls=%async_computation | async-start | bytes 393216 | tf_op jit(solution)/shard_map/all_to_all | solution.py:74
  19.7 1.1 fusion.1
  20.7 2.9 %collective-permute-start.1 = (bf16[2,64,768]{2,1,0:T(8,128)(2,1)S(1)}, bf16[2,64,768]{2,1,0:T(8,128)(2,1)S(1)}, u32[]{:S(2)}, u32[]{:S(2)}) collective-permute-start(bf16[2,64,768]{2,1,0:T(8,128)(2,1)S(1)} %get-tuple-element.13), channel_id=1, source_target_pairs={{4,0},{8,4},{12,8},{16,12},{20,16},{24,20},{28,24},{32,28},{36,32}... | collective-permute-start | bytes 589832 | tf_op jit(solution)/shard_map/ppermute | solution.py:94
  23.6 3.4 %collective-permute-start = (bf16[2,64,768]{2,1,0:T(8,128)(2,1)S(1)}, bf16[2,64,768]{2,1,0:T(8,128)(2,1)S(1)}, u32[]{:S(2)}, u32[]{:S(2)}) collective-permute-start(bf16[2,64,768]{2,1,0:T(8,128)(2,1)S(1)} %get-tuple-element.14), channel_id=1, source_target_pairs={{0,4},{4,8},{8,12},{12,16},{16,20},{20,24},{24,28},{28,32},{32,36}... | collective-permute-start | bytes 589832 | tf_op jit(solution)/shard_map/ppermute | solution.py:93
  27.1 0.0 copy-start.7
  27.2 4.1 %all-to-all-done = bf16[16,16,384]{2,1,0:T(8,128)(2,1)S(1)} async-done(((bf16[16,16,384]{2,1,0:T(8,128)(2,1)}), bf16[16,16,384]{2,1,0:T(8,128)(2,1)S(1)}, u32[]{:S(2)}, u32[]{:S(2)}) %all-to-all-start) | async-done | bytes 196640 | tf_op jit(solution)/shard_map/all_to_all | solution.py:74
  31.2 0.9 broadcast_in_dim.15
  32.2 4.0 %all-to-all-start.1 = ((bf16[4,256,384]{2,1,0:T(8,128)(2,1)}), bf16[4,256,384]{2,1,0:T(8,128)(2,1)S(1)}, u32[]{:S(2)}, u32[]{:S(2)}) async-start(bf16[4,256,384]{2,1,0:T(8,128)(2,1)} %broadcast_in_dim.15), calls=%async_computation.1 | async-start | bytes 1572864 | tf_op jit(solution)/shard_map/all_to_all | solution.py:74
  36.2 0.0 collective-permute-done.1.bottom_ref
  36.2 0.0 collective-permute-done.top_ref
  36.3 4.4 %collective-permute-start.2 = (bf16[8,2,768]{2,1,0:T(2,128)(2,1)S(1)}, bf16[8,2,768]{2,1,0:T(2,128)(2,1)S(1)}, u32[]{:S(2)}, u32[]{:S(2)}) collective-permute-start(bf16[8,2,768]{2,1,0:T(2,128)(2,1)S(1)} %pad_maximum_fusion.1), channel_id=1, source_target_pairs={{0,1},{1,2},{2,3},{4,5},{5,6},{6,7},{8,9},{9,10},{10,11},{12,13},{... | collective-permute-start | bytes 73736 | tf_op jit(solution)/shard_map/ppermute | solution.py:100
  40.7 7.3 %all-to-all-done.1 = bf16[4,256,384]{2,1,0:T(8,128)(2,1)S(1)} async-done(((bf16[4,256,384]{2,1,0:T(8,128)(2,1)}), bf16[4,256,384]{2,1,0:T(8,128)(2,1)S(1)}, u32[]{:S(2)}, u32[]{:S(2)}) %all-to-all-start.1) | async-done | bytes 786464 | tf_op jit(solution)/shard_map/all_to_all | solution.py:74
  48.0 5.4 %collective-permute-start.4 = (bf16[1024,384]{1,0:T(8,128)(2,1)S(1)}, bf16[1024,384]{1,0:T(8,128)(2,1)S(1)}, u32[]{:S(2)}, u32[]{:S(2)}) collective-permute-start(bf16[1024,384]{1,0:T(8,128)(2,1)S(1)} %bitcast.16), channel_id=1, source_target_pairs={{0,4},{4,0},{8,12},{12,8},{16,20},{20,16},{24,28},{28,24},{32,36},... | collective-permute-start | bytes 2359304 | tf_op jit(solution)/shard_map/ppermute | solution.py:85
  53.5 1.3 %collective-permute-start.3 = (bf16[8,2,768]{2,1,0:T(2,128)(2,1)S(1)}, bf16[8,2,768]{2,1,0:T(2,128)(2,1)S(1)}, u32[]{:S(2)}, u32[]{:S(2)}) collective-permute-start(bf16[8,2,768]{2,1,0:T(2,128)(2,1)S(1)} %pad_maximum_fusion.2), channel_id=1, source_target_pairs={{1,0},{2,1},{3,2},{5,4},{6,5},{7,6},{9,8},{10,9},{11,10},{13,12},{... | collective-permute-start | bytes 73736 | tf_op jit(solution)/shard_map/ppermute | solution.py:100
  54.8 0.1 add_convert_fusion.edge_ref
  54.9 0.0 collective-permute-done.2.west_ref
  54.9 4.6 %collective-permute-done.3.east_ref = bf16[8,2,768]{2,1,0:T(2,128)(2,1)S(1)} collective-permute-done((bf16[8,2,768]{2,1,0:T(2,128)(2,1)S(1)}, bf16[8,2,768]{2,1,0:T(2,128)(2,1)S(1)}, u32[]{:S(2)}, u32[]{:S(2)}) %collective-permute-start.3) | collective-permute-done | bytes 24608 | tf_op jit(solution)/shard_map/ppermute | solution.py:100
  59.4 9.8 %front.1 = (f32[6,528,96]{2,1,0:T(8,128)S(1)}, bf16[6,528,96]{2,1,0:T(8,128)(2,1)S(1)}) custom-call(bf16[4,64,768]{2,1,0:T(8,128)(2,1)S(1)} %copy-done, bf16[2,64,768]{2,1,0:T(8,128)(2,1)S(1)} %collective-permute-done.top_ref, bf16[2,64,768]{2,1,0:T(8,128)(2,1)S(1)} %collective-permute-done.1.bottom_ref, ...), custom_call_target="tpu_custom_call" | custom-call | flops 6000000000 | bytes 5000000 | tf_op jit(solution)/shard_map/front/pallas_call | solution.py:156
  69.2 1.2 %copy-done.3 = f32[6,528,96]{2,1,0:T(8,128)} copy-done((f32[6,528,96]{2,1,0:T(8,128)}, f32[6,528,96]{2,1,0:T(8,128)S(1)}, u32[]{:S(2)}) %copy-start.3) | copy-done | bytes 1216536
  70.4 0.0 collective-permute-done.4
  70.4 1.3 %pad_maximum_fusion.kv_ref = bf16[2048,384]{1,0:T(8,128)(2,1)} fusion(bf16[1024,384]{1,0:T(8,128)(2,1)S(1)} %collective-permute-done.4, bf16[1024,384]{1,0:T(8,128)(2,1)S(1)} %bitcast.17), kind=kLoop, calls=%fused_computation | loop fusion | flops 3145728 | bytes 3145728 | tf_op jit(solution)/shard_map/concatenate | solution.py:86
  71.7 39.3 %back.1 = bf16[4,64,768]{2,1,0:T(8,128)(2,1)} custom-call(s32[2]{0:T(128)S(1)} %add_convert_fusion.edge_ref, f32[6,528,96]{2,1,0:T(8,128)} %copy-done.3, bf16[6,528,96]{2,1,0:T(8,128)(2,1)S(1)} %get-tuple-element.8.q_ref, bf16[2048,384]{1,0:T(8,128)(2,1)} %pad_maximum_fusion.kv_ref, bf16[4,64,768]{2,1,0:T(8,128)(2,1)S(1)} %copy-done, ...), custom_call_target="tpu_custom_call" | custom-call | flops 20000000000 | bytes 6000000 | tf_op jit(solution)/shard_map/back/pallas_call | solution.py:269
  (22 shorter events, 0.2 us)
Async XLA Ops:
  0.0 27.1 %copy-start = (bf16[4,64,768]{2,1,0:T(8,128)(2,1)S(1)}, bf16[4,64,768]{2,1,0:T(8,128)(2,1)}, u32[]{:S(2)}) copy-start(bf16[4,64,768]{2,1,0:T(8,128)(2,1)} %field_ref.3) | copy-start | bytes 1179652
  0.0 27.0 %copy-start.5 = (bf16[2,96,96]{2,1,0:T(8,128)(2,1)S(1)}, bf16[2,96,96]{2,1,0:T(8,128)(2,1)}, u32[]{:S(2)}) copy-start(bf16[2,96,96]{2,1,0:T(8,128)(2,1)} %param.20) | copy-start | bytes 110596
  0.0 27.0 %copy-start.6 = (bf16[2,96,96]{2,1,0:T(8,128)(2,1)S(1)}, bf16[2,96,96]{2,1,0:T(8,128)(2,1)}, u32[]{:S(2)}) copy-start(bf16[2,96,96]{2,1,0:T(8,128)(2,1)} %param.19) | copy-start | bytes 110596
  0.0 27.1 %copy-start.4 = (bf16[2,9,96,96]{3,2,1,0:T(8,128)(2,1)S(1)}, bf16[2,9,96,96]{3,2,1,0:T(8,128)(2,1)}, u32[]{:S(2)}) copy-start(bf16[2,9,96,96]{3,2,1,0:T(8,128)(2,1)} %param.18) | copy-start | bytes 995332
  3.4 27.8 %all-to-all-start = ((bf16[16,16,384]{2,1,0:T(8,128)(2,1)}), bf16[16,16,384]{2,1,0:T(8,128)(2,1)S(1)}, u32[]{:S(2)}, u32[]{:S(2)}) async-start(bf16[16,16,384]{2,1,0:T(8,128)(2,1)} %broadcast_in_dim.6), calls=%async_computation | async-start | bytes 393216 | tf_op jit(solution)/shard_map/all_to_all | solution.py:74
  20.7 15.5 %collective-permute-start.1 = (bf16[2,64,768]{2,1,0:T(8,128)(2,1)S(1)}, bf16[2,64,768]{2,1,0:T(8,128)(2,1)S(1)}, u32[]{:S(2)}, u32[]{:S(2)}) collective-permute-start(bf16[2,64,768]{2,1,0:T(8,128)(2,1)S(1)} %get-tuple-element.13), channel_id=1, source_target_pairs={{4,0},{8,4},{12,8},{16,12},{20,16},{24,20},{28,24},{32,28},{36,32}... | collective-permute-start | bytes 589832 | tf_op jit(solution)/shard_map/ppermute | solution.py:94
  23.6 12.7 %collective-permute-start = (bf16[2,64,768]{2,1,0:T(8,128)(2,1)S(1)}, bf16[2,64,768]{2,1,0:T(8,128)(2,1)S(1)}, u32[]{:S(2)}, u32[]{:S(2)}) collective-permute-start(bf16[2,64,768]{2,1,0:T(8,128)(2,1)S(1)} %get-tuple-element.14), channel_id=1, source_target_pairs={{0,4},{4,8},{8,12},{12,16},{16,20},{20,24},{24,28},{28,32},{32,36}... | collective-permute-start | bytes 589832 | tf_op jit(solution)/shard_map/ppermute | solution.py:93
  27.1 9.1 %copy-start.7 = (f32[2,96]{1,0:T(2,128)S(1)}, f32[2,96]{1,0:T(2,128)}, u32[]{:S(2)}) copy-start(f32[2,96]{1,0:T(2,128)} %param.17) | copy-start | bytes 2308
  32.2 15.8 %all-to-all-start.1 = ((bf16[4,256,384]{2,1,0:T(8,128)(2,1)}), bf16[4,256,384]{2,1,0:T(8,128)(2,1)S(1)}, u32[]{:S(2)}, u32[]{:S(2)}) async-start(bf16[4,256,384]{2,1,0:T(8,128)(2,1)} %broadcast_in_dim.15), calls=%async_computation.1 | async-start | bytes 1572864 | tf_op jit(solution)/shard_map/all_to_all | solution.py:74
  36.3 18.6 %collective-permute-start.2 = (bf16[8,2,768]{2,1,0:T(2,128)(2,1)S(1)}, bf16[8,2,768]{2,1,0:T(2,128)(2,1)S(1)}, u32[]{:S(2)}, u32[]{:S(2)}) collective-permute-start(bf16[8,2,768]{2,1,0:T(2,128)(2,1)S(1)} %pad_maximum_fusion.1), channel_id=1, source_target_pairs={{0,1},{1,2},{2,3},{4,5},{5,6},{6,7},{8,9},{9,10},{10,11},{12,13},{... | collective-permute-start | bytes 73736 | tf_op jit(solution)/shard_map/ppermute | solution.py:100
  48.0 22.4 %collective-permute-start.4 = (bf16[1024,384]{1,0:T(8,128)(2,1)S(1)}, bf16[1024,384]{1,0:T(8,128)(2,1)S(1)}, u32[]{:S(2)}, u32[]{:S(2)}) collective-permute-start(bf16[1024,384]{1,0:T(8,128)(2,1)S(1)} %bitcast.16), channel_id=1, source_target_pairs={{0,4},{4,0},{8,12},{12,8},{16,20},{20,16},{24,28},{28,24},{32,36},... | collective-permute-start | bytes 2359304 | tf_op jit(solution)/shard_map/ppermute | solution.py:85
  53.5 5.9 %collective-permute-start.3 = (bf16[8,2,768]{2,1,0:T(2,128)(2,1)S(1)}, bf16[8,2,768]{2,1,0:T(2,128)(2,1)S(1)}, u32[]{:S(2)}, u32[]{:S(2)}) collective-permute-start(bf16[8,2,768]{2,1,0:T(2,128)(2,1)S(1)} %pad_maximum_fusion.2), channel_id=1, source_target_pairs={{1,0},{2,1},{3,2},{5,4},{6,5},{7,6},{9,8},{10,9},{11,10},{13,12},{... | collective-permute-start | bytes 73736 | tf_op jit(solution)/shard_map/ppermute | solution.py:100
  69.2 1.2 %copy-start.3 = (f32[6,528,96]{2,1,0:T(8,128)}, f32[6,528,96]{2,1,0:T(8,128)S(1)}, u32[]{:S(2)}) copy-start(f32[6,528,96]{2,1,0:T(8,128)S(1)} %get-tuple-element.7.acc_ref) | copy-start | bytes 3649540
  70.4 1.3 %copy-start.1 = (bf16[4,64,768]{2,1,0:T(8,128)(2,1)S(1)}, bf16[4,64,768]{2,1,0:T(8,128)(2,1)}, u32[]{:S(2)}) copy-start(bf16[4,64,768]{2,1,0:T(8,128)(2,1)} %noise_ref.1) | copy-start | bytes 1179652
  70.4 1.3 %copy-start.2 = (bf16[2,96,96]{2,1,0:T(8,128)(2,1)S(1)}, bf16[2,96,96]{2,1,0:T(8,128)(2,1)}, u32[]{:S(2)}) copy-start(bf16[2,96,96]{2,1,0:T(8,128)(2,1)} %out_ref.1) | copy-start | bytes 110596

commit v2 on v1

v2 whole, which is shorter than its diff:
```python
import math

import jax
import jax.numpy as jnp
from jax import lax
from jax.experimental import pallas as pl
from jax.experimental.pallas import tpu as pltpu
from jax.sharding import PartitionSpec as P

C = 96
LATENT = 512
TYPES = 8
HEADS = 2
BLOCKS = 2
LAYERS = 8
HDIM = 48
LANES = 128
EPS = 1e-06
SCORE_SCALE = 1.0 / math.sqrt(HDIM) * math.log2(math.e)
SAFE_SCORE = 96.0
TILE = 1024

F32 = jnp.float32
BF16 = jnp.bfloat16


def dot(a, b):
    return jnp.dot(a, b, preferred_element_type=F32)


def silu(x):
    return 0.5 * x * (1.0 + jnp.tanh(0.5 * x))


def tokens_kernel(type_ref, latent_ref, table_ref, weight_ref, kv_ref):
    rows = latent_ref.shape[0]
    row = lax.broadcasted_iota(jnp.int32, (rows, TYPES), 0)
    column = lax.broadcasted_iota(jnp.int32, (rows, TYPES), 1)
    kind = jnp.zeros((rows, TYPES), jnp.int32)
    for i in range(rows):
        kind = jnp.where(row == i, type_ref[i], kind)
    picked = (kind == column).astype(F32).astype(BF16)
    embed = dot(picked, table_ref[...])
    hidden = jax.nn.silu(latent_ref[...].astype(F32) + embed).astype(BF16)
    kv = dot(hidden, weight_ref[...]).astype(BF16)
    for i in range(kv_ref.shape[0]):
        kv_ref[i] = kv


def local_tokens(coarse_latent, particle_type, type_table, kv_weight, copies):
    vmem = pl.BlockSpec(memory_space=pltpu.VMEM)
    return pl.pallas_call(
        tokens_kernel,
        out_shape=jax.ShapeDtypeStruct(
            (copies, coarse_latent.shape[0], kv_weight.shape[1]), BF16
        ),
        in_specs=[pl.BlockSpec(memory_space=pltpu.SMEM), vmem, vmem, vmem],
        out_specs=vmem,
        cost_estimate=pl.CostEstimate(flops=6_000_000, bytes_accessed=700_000, transcendentals=8192),
        name="tokens",
    )(particle_type, coarse_latent, type_table, kv_weight)


def phi_index(x, y, z, core):
    return ((x * 2 + y) * 8 + z) * 2 + core


YZ_GROUPS = [
    [phi_index(x, y, z, c) for y in range(2) for z in range(8)] for x in range(4) for c in range(2)
]
X_GROUPS = [
    [phi_index(x, y, z, c) for x in range(4)] for y in range(2) for z in range(8) for c in range(2)
]


def exchange(copies, groups):
    rows = lax.all_to_all(copies, "phi", 0, 0, tiled=True, axis_index_groups=groups)
    return rows.reshape(-1, rows.shape[-1])


def halo_phi(field):
    count = lax.axis_size("phi")
    up = [(i, (i + 1) % count) for i in range(count)]
    down = [((i + 1) % count, i) for i in range(count)]
    return lax.ppermute(field[-2:], "phi", up), lax.ppermute(field[:2], "phi", down)


def halo_eta(field, top, bottom):
    bands = lax.axis_size("eta")
    right = [(i, i + 1) for i in range(bands - 1)]
    left = [(i + 1, i) for i in range(bands - 1)]
    west = jnp.concatenate([top[:, -2:], field[:, -2:], bottom[:, -2:]], axis=0)
    east = jnp.concatenate([top[:, :2], field[:, :2], bottom[:, :2]], axis=0)
    return lax.ppermute(west, "eta", right), lax.ppermute(east, "eta", left)


def normalized(x, gain):
    mean = jnp.sum(x * x, axis=-1, keepdims=True) * (1.0 / C)
    return x * lax.rsqrt(mean + EPS) * gain


def widened(x):
    return jnp.concatenate([x, jnp.zeros((x.shape[0], LANES - C), x.dtype)], axis=1)


def keep_taps(normed, row, outer, centre):
    outer[row] = normed.astype(BF16)
    centre[row] = normed[LAYERS:-LAYERS].astype(BF16)


def pack_weight(weight_ref, block, packed):
    packed[...] = jnp.zeros_like(packed)
    for tap in range(9):
        packed[tap * LANES : tap * LANES + C, :] = weight_ref[block, tap]


def conv_branch(outer, centre, row, length, packed, mix):
    taps = []
    for di in range(3):
        taps.append(outer[row + di, 0:length, :])
        taps.append(centre[row + di, 0:length, :])
        taps.append(outer[row + di, 2 * LAYERS : 2 * LAYERS + length, :])
    conv = dot(jnp.concatenate(taps, axis=1), packed[...])
    return dot(silu(conv).astype(BF16), mix)


def front_kernel(
    field_ref, top_ref, bottom_ref, west_ref, east_ref, gain_ref, conv_ref, query_ref, mix_ref,
    acc_ref, q_ref, done_ref, cells, outer, centre, packed, acc, queries, sems,
):
    span_p, span_e = field_ref.shape[0], field_ref.shape[1]
    length = (span_e + 2) * LAYERS
    gain = widened(gain_ref[0:1, :])
    pack_weight(conv_ref, 0, packed)

    def put(row, start, piece):
        count = piece.shape[0]
        for layer in range(LAYERS):
            part = piece[:, layer * C : (layer + 1) * C]
            cells[row, pl.ds(start * LAYERS + layer, count, stride=LAYERS), :] = widened(part)

    for row in range(span_p + 4):
        if row < 2:
            middle = top_ref[row]
        elif row < span_p + 2:
            middle = field_ref[row - 2]
        else:
            middle = bottom_ref[row - span_p - 2]
        put(row, 2, middle.astype(F32))
        put(row, 0, west_ref[row].astype(F32))
        put(row, span_e + 2, east_ref[row].astype(F32))
        keep_taps(normalized(cells[row], gain), row, outer, centre)
    copies = []
    for row in range(span_p + 2):
        branch = conv_branch(outer, centre, row, length, packed, mix_ref[0])
        acc[row] = cells[row + 1, LAYERS : LAYERS + length, :][:, :C] + branch
        q = dot(centre[row + 1][:, :C], query_ref[0])
        span = slice(row * length, (row + 1) * length)
        queries[span, :] = q.astype(BF16)
        copies.append(pltpu.make_async_copy(acc.at[row], acc_ref.at[row], sems.at[0, row]))
        copies.append(pltpu.make_async_copy(queries.at[span], q_ref.at[span], sems.at[1, row]))
        copies[-2].start()
        copies[-1].start()
    for copy in copies:
        copy.wait()
    done_ref[...] = jnp.zeros_like(done_ref)


def front(field, top, bottom, west, east, gain, conv_weight, query_weight, mix_weight):
    span_p, span_e = field.shape[0], field.shape[1]
    vmem = pl.BlockSpec(memory_space=pltpu.VMEM)
    rows, width = span_p + 2, (span_e + 2) * LAYERS
    return pl.pallas_call(
        front_kernel,
        out_shape=[
            jax.ShapeDtypeStruct((rows, width, C), F32),
            jax.ShapeDtypeStruct((rows * width, C), BF16),
            jax.ShapeDtypeStruct((8, LANES), BF16),
        ],
        in_specs=[vmem] * 9,
        out_specs=[pl.BlockSpec(memory_space=pltpu.HBM)] * 2 + [vmem],
        scratch_shapes=[
            pltpu.VMEM((rows + 2, width + 2 * LAYERS, LANES), F32),
            pltpu.VMEM((rows + 2, width + 2 * LAYERS, LANES), BF16),
            pltpu.VMEM((rows + 2, width, LANES), BF16),
            pltpu.VMEM((9 * LANES, C), BF16),
            pltpu.VMEM((rows, width, C), F32),
            pltpu.VMEM((rows * width, C), BF16),
            pltpu.SemaphoreType.DMA((2, rows)),
        ],
        compiler_params=pltpu.CompilerParams(vmem_limit_bytes=60 * 1024 * 1024),
        cost_estimate=pl.CostEstimate(
            flops=6_000_000_000, bytes_accessed=5_000_000, transcendentals=400_000
        ),
        name="front",
    )(field, top, bottom, west, east, gain, conv_weight, query_weight, mix_weight)


def prepare_tokens(kv_refs, keys, values):
    tokens = kv_refs[0].shape[0]
    largest = [[0.0] * HEADS for _ in range(BLOCKS)]
    pad = values.shape[2] - HDIM
    ones = (lax.broadcasted_iota(jnp.int32, (pad, tokens), 0) == 0).astype(F32).astype(BF16)
    for part, kv_ref in enumerate(kv_refs):
        span = slice(part * tokens, (part + 1) * tokens)
        turned = jnp.transpose(kv_ref[...])
        for block in range(BLOCKS):
            start = 2 * C * block
            keys[block, span, :] = kv_ref[:, start : start + C]
            for head in range(HEADS):
                low = start + head * HDIM
                key = turned[low : low + HDIM].astype(F32)
                longest = jnp.max(jnp.sum(key * key, axis=0, keepdims=True))
                largest[block][head] = jnp.maximum(largest[block][head], longest)
                values[block, head, 0:HDIM, span] = turned[low + C : low + C + HDIM]
                values[block, head, HDIM : HDIM + pad, span] = ones
    return largest


def attend(q, keys, values, safe):
    head_row = lax.broadcasted_iota(jnp.int32, q.shape, 0)
    results = []
    for head in range(HEADS):
        mine = (head_row >= head * HDIM) & (head_row < (head + 1) * HDIM)
        scores = dot(keys[...], jnp.where(mine, q, jnp.zeros_like(q)))
        if not safe:
            scores = scores - jnp.max(scores, axis=0, keepdims=True)
        probs = jnp.exp2(scores * SCORE_SCALE).astype(BF16)
        out = dot(values[head], probs)
        results.append(out[:HDIM] * (1.0 / out[HDIM : HDIM + 1]))
    return jnp.concatenate(results, axis=0).astype(BF16)


def within(q, largest):
    square = q.astype(F32)
    square = square * square
    worst = [
        jnp.max(jnp.sum(square[h * HDIM : (h + 1) * HDIM], axis=0, keepdims=True)) * largest[h]
        for h in range(HEADS)
    ]
    return jnp.maximum(worst[0], worst[1]) <= (SAFE_SCORE / SCORE_SCALE) ** 2


def back_kernel(
    edge_ref, _, acc_ref, q_ref, kv_ref, other_ref, field_in, noise_in, gain_ref, conv_ref,
    query_ref, mix_ref, out_ref, result_ref, keys, values, attended, second, stream, outer, centre,
    packed, flat, acc, queries, field_ref, noise_ref, sems,
):
    span_p, span_e = field_ref.shape[0], field_ref.shape[1]
    width, inner = (span_e + 2) * LAYERS, span_e * LAYERS
    q_copy = pltpu.make_async_copy(q_ref, queries, sems.at[0])
    acc_copy = pltpu.make_async_copy(acc_ref, acc, sems.at[1])
    late = [
        pltpu.make_async_copy(field_in, field_ref, sems.at[2]),
        pltpu.make_async_copy(noise_in, noise_ref, sems.at[3]),
    ]
    for copy in [q_copy, acc_copy] + late:
        copy.start()
    gain = widened(gain_ref[1:2, :])
    largest = prepare_tokens([kv_ref, other_ref], keys, values)
    pack_weight(conv_ref, 1, packed)

    def attend_rows(source, block, start, rows):
        q = jnp.transpose(source[pl.ds(start, rows), :])
        fine = within(q, largest[block])

        def go(safe):
            found = attend(q, keys.at[block], values.at[block], safe)
            attended[pl.ds(start, rows), :] = jnp.transpose(found)

        pl.when(fine)(lambda: go(True))
        pl.when(jnp.logical_not(fine))(lambda: go(False))

    def attend_all(source, block, count):
        tiles = count // TILE

        @pl.loop(0, tiles)
        def _(tile):
            attend_rows(source, block, pl.multiple_of(tile * TILE, TILE), TILE)

        rest = count - tiles * TILE
        if rest:
            rest = -(-rest // LANES) * LANES
            attend_rows(source, block, count - rest, rest)

    q_copy.wait()
    attend_all(queries, 0, (span_p + 2) * width)
    acc_copy.wait()
    for row in range(span_p + 2):
        branch = dot(attended[row * width : (row + 1) * width, :], out_ref[0])
        new = acc[row] + branch
        if 0 < row < span_p + 1:
            stream[row - 1] = new[LAYERS:-LAYERS]
        place = lax.broadcasted_iota(jnp.int32, new.shape, 0)
        outside = ((place < LAYERS) & (edge_ref[0] == 1)) | (
            (place >= width - LAYERS) & (edge_ref[1] == 1)
        )
        normed = normalized(widened(jnp.where(outside, 0.0, new)), gain)
        keep_taps(normed, row, outer, centre)
        if 0 < row < span_p + 1:
            q = dot(centre[row][:, :C], query_ref[1])
            second[(row - 1) * inner : row * inner, :] = q.astype(BF16)

    attend_all(second, 1, span_p * inner)
    for copy in late:
        copy.wait()
    for row in range(span_p):
        branch = conv_branch(outer, centre, row, inner, packed, mix_ref[1])
        new = stream[row] + branch + dot(attended[row * inner : (row + 1) * inner, :], out_ref[1])
        flat[...] = widened(new)
        for layer in range(LAYERS):
            last = flat[pl.ds(layer, span_e, stride=LAYERS), :][:, :C]
            span = slice(layer * C, (layer + 1) * C)
            field = field_ref[row, :, span].astype(F32)
            noise = noise_ref[row, :, span].astype(F32)
            result_ref[row, :, span] = (1.02 * (field - 0.2 * last) + 0.3 * noise).astype(BF16)


def back(edges, done, acc, q, kv, other, field, noise, gain, conv_weight, query_weight, mix_weight, out_weight):
    span_p, span_e = field.shape[0], field.shape[1]
    vmem = pl.BlockSpec(memory_space=pltpu.VMEM)
    tokens = kv.shape[0] + other.shape[0]
    rows, width, inner = span_p + 2, (span_e + 2) * LAYERS, span_e * LAYERS
    return pl.pallas_call(
        back_kernel,
        out_shape=jax.ShapeDtypeStruct(field.shape, BF16),
        in_specs=[pl.BlockSpec(memory_space=pltpu.SMEM), pl.BlockSpec(memory_space=pl.ANY)]
        + [pl.BlockSpec(memory_space=pltpu.HBM)] * 2
        + [vmem] * 2
        + [pl.BlockSpec(memory_space=pl.ANY)] * 2
        + [vmem] * 5,
        out_specs=vmem,
        scratch_shapes=[
            pltpu.VMEM((BLOCKS, tokens, C), BF16),
            pltpu.VMEM((BLOCKS, HEADS, 64, tokens), BF16),
            pltpu.VMEM((rows * width, C), BF16),
            pltpu.VMEM((span_p * inner, C), BF16),
            pltpu.VMEM((span_p, inner, C), F32),
            pltpu.VMEM((rows, width, LANES), BF16),
            pltpu.VMEM((rows, inner, LANES), BF16),
            pltpu.VMEM((9 * LANES, C), BF16),
            pltpu.VMEM((inner, LANES), F32),
            pltpu.VMEM((rows, width, C), F32),
            pltpu.VMEM((rows * width, C), BF16),
            pltpu.VMEM(field.shape, BF16),
            pltpu.VMEM(field.shape, BF16),
            pltpu.SemaphoreType.DMA((4,)),
        ],
        compiler_params=pltpu.CompilerParams(vmem_limit_bytes=60 * 1024 * 1024),
        cost_estimate=pl.CostEstimate(
            flops=20_000_000_000, bytes_accessed=6_000_000, transcendentals=21_000_000
        ),
        name="back",
    )(edges, done, acc, q, kv, other, field, noise, gain, conv_weight, query_weight, mix_weight, out_weight)


def tokens_and_front(
    coarse_latent, particle_type, type_table, kv_weight, field, gain, conv_weight, query_weight,
    mix_weight,
):
    local = local_tokens(coarse_latent, particle_type, type_table, kv_weight, len(YZ_GROUPS[0]))
    top, bottom = halo_phi(field)
    west, east = halo_eta(field, top, bottom)
    kv = exchange(local, YZ_GROUPS)
    kv, west, east = lax.optimization_barrier((kv, west, east))
    acc, q, done = front(
        field, top, bottom, west, east, gain, conv_weight, query_weight, mix_weight
    )
    copies = jnp.broadcast_to(kv[None], (len(X_GROUPS[0]),) + kv.shape)
    kv = exchange(copies, X_GROUPS)
    kv, done = lax.optimization_barrier((kv, done))
    other = lax.ppermute(kv, "phi", [(i, i ^ 1) for i in range(lax.axis_size("phi"))])
    return kv, other, acc, q, done


def body(
    noisy_field,
    noise_draw,
    coarse_latent,
    particle_type,
    type_table,
    kv_weight,
    norm_gain,
    conv_weight,
    query_weight,
    mix_weight,
    out_weight,
):
    kv, other, acc, q, done = tokens_and_front(
        coarse_latent, particle_type, type_table, kv_weight, noisy_field, norm_gain, conv_weight,
        query_weight, mix_weight,
    )
    band = lax.axis_index("eta")
    edges = jnp.stack([band == 0, band == lax.axis_size("eta") - 1]).astype(jnp.int32)
    return back(
        edges, done, acc, q, kv, other, noisy_field, noise_draw, norm_gain, conv_weight, query_weight,
        mix_weight, out_weight,
    )


def solution(mesh):
    in_specs = (
        P("phi", "eta", None),
        P("phi", "eta", None),
        P("phi", None),
        P("phi"),
        P(),
        P(),
        P(),
        P(),
        P(),
        P(),
        P(),
    )
    out_specs = P("phi", "eta", None)
    return jax.shard_map(body, mesh=mesh, in_specs=in_specs, out_specs=out_specs, check_vma=False)
```

time: 112 us -> 101 us (0.902); the launches traced: 111 us -> 98.8 us
  Pallas kernels: 51.1 us -> 43.3 us
  waiting for transfers between devices: 15.9 us -> 9.59 us
  starting transfers between devices: 37.6 us -> 41.2 us
    all_to_all x2, waiting for transfers between devices: 11.4 us -> 0.01 us  [exchange(): lax.all_to_all(copies, 'phi', 0, 0, tiled=True, axis_index_groups=groups)]
    pallas_call x1, Pallas kernels: 39.3 us -> 32.1 us  [back(): pl.pallas_call(back_kernel, out_shape=jax.ShapeDtypeStruct(field.shape, B...]
    ppermute x5, waiting for transfers between devices: 4.57 us -> 9.58 us  [the longest x2 3.58 us: halo_eta(): return (lax.ppermute(west, 'eta', right), lax.ppermute(east, 'eta', left))]
    ppermute x5, starting transfers between devices: 17.4 us -> 21.3 us  [the longest x1 10.3 us: tokens_and_front(): lax.ppermute(kv, 'phi', [(i, i ^ 1) for i in range(lax.axis_size('phi'))])]
    broadcast_in_dim x2 -> x1, local copies, waits for them, and re-layouts: 2.35 us -> 0.97 us  [tokens_and_front(): copies = jnp.broadcast_to(kv[None], (len(X_GROUPS[0]),) + kv.shape)]
    concatenate x3 -> x2, other arithmetic: 1.39 us -> 0.08 us  [the longest x1 0.04 us: halo_eta(): east = jnp.concatenate([top[:, :2], field[:, :2], bottom[:, :2]], axis=0)]
  transfers between devices with their start and end apart: 7 -> 7, of which waited for: 3 -> 4; matrix products, arithmetic and copies ran while one was open for 2% -> 3% of each run, Pallas kernels for 9% -> 9%
where the time goes in v2:
time: 101 us; the launch traced here: 98.8 us
  Pallas kernels  43.3 us (43%)
  starting transfers between devices  41.2 us (41%)
  waiting for transfers between devices  9.59 us (9%)
  local copies, waits for them, and re-layouts  3.8 us (4%)
    pallas_call x1, Pallas kernels, back(): pl.pallas_call(back_kernel, out_shape=jax.ShapeDtypeStruct(field.shape, B...  32.1 us
    all_to_all x2, starting transfers between devices, exchange(): lax.all_to_all(copies, 'phi', 0, 0, tiled=True, axis_index_groups=groups)  19.9 us
    ppermute x1, starting transfers between devices, tokens_and_front(): lax.ppermute(kv, 'phi', [(i, i ^ 1) for i in range(lax.axis_size('phi'))])  10.3 us
    pallas_call x1, Pallas kernels, front(): pl.pallas_call(front_kernel, out_shape=[jax.ShapeDtypeStruct((rows, width...  9.16 us
    ppermute x2, starting transfers between devices, halo_eta(): return (lax.ppermute(west, 'eta', right), lax.ppermute(east, 'eta', left))  4.69 us
    ppermute x1, starting transfers between devices, halo_phi(): lax.ppermute(field[-2:], 'phi', up)  4.39 us
    ppermute x2, waiting for transfers between devices, halo_eta(): return (lax.ppermute(west, 'eta', right), lax.ppermute(east, 'eta', left))  3.58 us
    ppermute x1, waiting for transfers between devices, halo_phi(): lax.ppermute(field[:2], 'phi', down)  3.44 us
  transfers between devices with their start and end apart: 7, of which 4 were waited for; matrix products, arithmetic and copies ran while one was open for 3% of the time, Pallas kernels for 9%

profile of v2, /device:TPU:1, one launch (start us, length us, event | category | flops | bytes accessed | tf_op | source)
XLA Modules:
  0.0 98.8 jit_solution(4123601228976936940)
XLA Ops:
  0.0 2.0 %tokens.1 = bf16[16,16,384]{2,1,0:T(8,128)(2,1)} custom-call(s32[16]{0:T(128)} %type_ref.1, bf16[16,512]{1,0:T(8,128)(2,1)} %latent_ref.1, bf16[8,512]{1,0:T(8,128)(2,1)} %table_ref.1, bf16[512,384]{1,0:T(8,128)(2,1)} %weight_ref.1), custom_call_target="tpu_custom_call" | custom-call | flops 6000000 | bytes 700000 | tf_op jit(solution)/shard_map/tokens/pallas_call | solution.py:52
  2.0 16.2 %all-to-all-start = ((bf16[16,16,384]{2,1,0:T(8,128)(2,1)}), bf16[16,16,384]{2,1,0:T(8,128)(2,1)S(1)}, u32[]{:S(2)}, u32[]{:S(2)}) async-start(bf16[16,16,384]{2,1,0:T(8,128)(2,1)} %tokens.1), calls=%async_computation | async-start | bytes 393216 | tf_op jit(solution)/shard_map/all_to_all | solution.py:77
  18.2 1.1 %fusion.1 = (bf16[2,64,768]{2,1,0:T(8,128)(2,1)S(1)}, bf16[2,64,768]{2,1,0:T(8,128)(2,1)S(1)}) fusion(bf16[4,64,768]{2,1,0:T(8,128)(2,1)} %field_in.1), kind=kLoop, calls=%fused_computation.4 | loop fusion | bytes 786432 | tf_op jit(solution)/shard_map/slice | solution.py:85
  19.3 4.4 %collective-permute-start = (bf16[2,64,768]{2,1,0:T(8,128)(2,1)S(1)}, bf16[2,64,768]{2,1,0:T(8,128)(2,1)S(1)}, u32[]{:S(2)}, u32[]{:S(2)}) collective-permute-start(bf16[2,64,768]{2,1,0:T(8,128)(2,1)S(1)} %get-tuple-element.23), channel_id=1, source_target_pairs={{0,4},{4,8},{8,12},{12,16},{16,20},{20,24},{24,28},{28,32},{32,36}... | collective-permute-start | bytes 589832 | tf_op jit(solution)/shard_map/ppermute | solution.py:85
  23.7 1.9 %collective-permute-start.1 = (bf16[2,64,768]{2,1,0:T(8,128)(2,1)S(1)}, bf16[2,64,768]{2,1,0:T(8,128)(2,1)S(1)}, u32[]{:S(2)}, u32[]{:S(2)}) collective-permute-start(bf16[2,64,768]{2,1,0:T(8,128)(2,1)S(1)} %get-tuple-element.24), channel_id=1, source_target_pairs={{4,0},{8,4},{12,8},{16,12},{20,16},{24,20},{28,24},{32,28},{36,32}... | collective-permute-start | bytes 589832 | tf_op jit(solution)/shard_map/ppermute | solution.py:85
  25.6 0.8 fusion
  26.5 1.4 %collective-permute-done.top_ref = bf16[2,64,768]{2,1,0:T(8,128)(2,1)S(1)} collective-permute-done((bf16[2,64,768]{2,1,0:T(8,128)(2,1)S(1)}, bf16[2,64,768]{2,1,0:T(8,128)(2,1)S(1)}, u32[]{:S(2)}, u32[]{:S(2)}) %collective-permute-start) | collective-permute-done | bytes 196640 | tf_op jit(solution)/shard_map/ppermute | solution.py:85
  27.9 3.4 %collective-permute-done.1.bottom_ref = bf16[2,64,768]{2,1,0:T(8,128)(2,1)S(1)} collective-permute-done((bf16[2,64,768]{2,1,0:T(8,128)(2,1)S(1)}, bf16[2,64,768]{2,1,0:T(8,128)(2,1)S(1)}, u32[]{:S(2)}, u32[]{:S(2)}) %collective-permute-start.1) | collective-permute-done | bytes 196640 | tf_op jit(solution)/shard_map/ppermute | solution.py:85
  31.4 3.4 %collective-permute-start.2 = (bf16[8,2,768]{2,1,0:T(2,128)(2,1)S(1)}, bf16[8,2,768]{2,1,0:T(2,128)(2,1)S(1)}, u32[]{:S(2)}, u32[]{:S(2)}) collective-permute-start(bf16[8,2,768]{2,1,0:T(2,128)(2,1)S(1)} %pad_maximum_fusion), channel_id=1, source_target_pairs={{0,1},{1,2},{2,3},{4,5},{5,6},{6,7},{8,9},{9,10},{10,11},{12,13},{... | collective-permute-start | bytes 73736 | tf_op jit(solution)/shard_map/ppermute | solution.py:94
  34.9 1.3 %collective-permute-start.3 = (bf16[8,2,768]{2,1,0:T(2,128)(2,1)S(1)}, bf16[8,2,768]{2,1,0:T(2,128)(2,1)S(1)}, u32[]{:S(2)}, u32[]{:S(2)}) collective-permute-start(bf16[8,2,768]{2,1,0:T(2,128)(2,1)S(1)} %pad_maximum_fusion.1), channel_id=1, source_target_pairs={{1,0},{2,1},{3,2},{5,4},{6,5},{7,6},{9,8},{10,9},{11,10},{13,12},{... | collective-permute-start | bytes 73736 | tf_op jit(solution)/shard_map/ppermute | solution.py:94
  36.2 0.0 collective-permute-done.2.west_ref
  36.2 3.6 %collective-permute-done.3.east_ref = bf16[8,2,768]{2,1,0:T(2,128)(2,1)S(1)} collective-permute-done((bf16[8,2,768]{2,1,0:T(2,128)(2,1)S(1)}, bf16[8,2,768]{2,1,0:T(2,128)(2,1)S(1)}, u32[]{:S(2)}, u32[]{:S(2)}) %collective-permute-start.3) | collective-permute-done | bytes 24608 | tf_op jit(solution)/shard_map/ppermute | solution.py:94
  39.8 0.0 all-to-all-done
  39.8 1.0 broadcast_in_dim.2
  40.8 3.7 %all-to-all-start.1 = ((bf16[4,256,384]{2,1,0:T(8,128)(2,1)}), bf16[4,256,384]{2,1,0:T(8,128)(2,1)S(1)}, u32[]{:S(2)}, u32[]{:S(2)}) async-start(bf16[4,256,384]{2,1,0:T(8,128)(2,1)} %broadcast_in_dim.2), calls=%async_computation.1 | async-start | bytes 1572864 | tf_op jit(solution)/shard_map/all_to_all | solution.py:77
  44.5 0.0 copy-done.4
  44.5 0.0 copy-done.5
  44.5 9.2 %front.1 = (f32[6,528,96]{2,1,0:T(8,128)}, bf16[3168,96]{1,0:T(8,128)(2,1)}, bf16[8,128]{1,0:T(8,128)(2,1)}) custom-call(bf16[4,64,768]{2,1,0:T(8,128)(2,1)} %field_in.1, bf16[2,64,768]{2,1,0:T(8,128)(2,1)} %copy-done.1, bf16[2,64,768]{2,1,0:T(8,128)(2,1)} %copy-done.2, bf16[8,2,768]{2,1,0:T(2,128)(2,1)} %copy-done.4, bf16[8,2,768]{2,1,0:T(2,128)(2,1)} %copy-done.5, ...), custom_call_target="tpu_custom_call" | custom-call | flops 6000000000 | bytes 5000000 | tf_op jit(solution)/shard_map/front/pallas_call | solution.py:173
  53.6 0.0 all-to-all-done.1
  53.7 10.3 %collective-permute-start.4 = (bf16[1024,384]{1,0:T(8,128)(2,1)S(1)}, bf16[1024,384]{1,0:T(8,128)(2,1)S(1)}, u32[]{:S(2)}, u32[]{:S(2)}) collective-permute-start(bf16[1024,384]{1,0:T(8,128)(2,1)S(1)} %bitcast.4), channel_id=1, source_target_pairs={{0,4},{4,0},{8,12},{12,8},{16,20},{20,16},{24,28},{28,24},{32,36},... | collective-permute-start | bytes 2359304 | tf_op jit(solution)/shard_map/ppermute | solution.py:372
  63.9 0.6 add_convert_fusion.edge_ref
  64.5 1.1 %collective-permute-done.4.other_ref = bf16[1024,384]{1,0:T(8,128)(2,1)S(1)} collective-permute-done((bf16[1024,384]{1,0:T(8,128)(2,1)S(1)}, bf16[1024,384]{1,0:T(8,128)(2,1)S(1)}, u32[]{:S(2)}, u32[]{:S(2)}) %collective-permute-start.4) | collective-permute-done | bytes 786464 | tf_op jit(solution)/shard_map/ppermute | solution.py:372
  65.7 0.9 copy-done.3
  66.5 32.1 %back.1 = bf16[4,64,768]{2,1,0:T(8,128)(2,1)} custom-call(s32[2]{0:T(128)} %add_convert_fusion.edge_ref, bf16[8,128]{1,0:T(8,128)(2,1)} %get-tuple-element.17._, f32[6,528,96]{2,1,0:T(8,128)} %get-tuple-element.18.acc_ref, bf16[3168,96]{1,0:T(8,128)(2,1)} %get-tuple-element.19.q_ref, bf16[1024,384]{1,0:T(8,128)(2,1)} %bitcast.5, ...), custom_call_target="tpu_custom_call" | custom-call | flops 20000000000 | bytes 6000000 | tf_op jit(solution)/shard_map/back/pallas_call | solution.py:324
  (13 shorter events, 0.1 us)
Async XLA Ops:
  2.0 37.8 %all-to-all-start = ((bf16[16,16,384]{2,1,0:T(8,128)(2,1)}), bf16[16,16,384]{2,1,0:T(8,128)(2,1)S(1)}, u32[]{:S(2)}, u32[]{:S(2)}) async-start(bf16[16,16,384]{2,1,0:T(8,128)(2,1)} %tokens.1), calls=%async_computation | async-start | bytes 393216 | tf_op jit(solution)/shard_map/all_to_all | solution.py:77
  19.3 8.6 %collective-permute-start = (bf16[2,64,768]{2,1,0:T(8,128)(2,1)S(1)}, bf16[2,64,768]{2,1,0:T(8,128)(2,1)S(1)}, u32[]{:S(2)}, u32[]{:S(2)}) collective-permute-start(bf16[2,64,768]{2,1,0:T(8,128)(2,1)S(1)} %get-tuple-element.23), channel_id=1, source_target_pairs={{0,4},{4,8},{8,12},{12,16},{16,20},{20,24},{24,28},{28,32},{32,36}... | collective-permute-start | bytes 589832 | tf_op jit(solution)/shard_map/ppermute | solution.py:85
  23.7 7.7 %collective-permute-start.1 = (bf16[2,64,768]{2,1,0:T(8,128)(2,1)S(1)}, bf16[2,64,768]{2,1,0:T(8,128)(2,1)S(1)}, u32[]{:S(2)}, u32[]{:S(2)}) collective-permute-start(bf16[2,64,768]{2,1,0:T(8,128)(2,1)S(1)} %get-tuple-element.24), channel_id=1, source_target_pairs={{4,0},{8,4},{12,8},{16,12},{20,16},{24,20},{28,24},{32,28},{36,32}... | collective-permute-start | bytes 589832 | tf_op jit(solution)/shard_map/ppermute | solution.py:85
  27.9 16.5 %copy-start.1 = (bf16[2,64,768]{2,1,0:T(8,128)(2,1)}, bf16[2,64,768]{2,1,0:T(8,128)(2,1)S(1)}, u32[]{:S(2)}) copy-start(bf16[2,64,768]{2,1,0:T(8,128)(2,1)S(1)} %collective-permute-done.top_ref) | copy-start | bytes 589828
  31.4 13.1 %copy-start.2 = (bf16[2,64,768]{2,1,0:T(8,128)(2,1)}, bf16[2,64,768]{2,1,0:T(8,128)(2,1)S(1)}, u32[]{:S(2)}) copy-start(bf16[2,64,768]{2,1,0:T(8,128)(2,1)S(1)} %collective-permute-done.1.bottom_ref) | copy-start | bytes 589828
  31.4 4.8 %collective-permute-start.2 = (bf16[8,2,768]{2,1,0:T(2,128)(2,1)S(1)}, bf16[8,2,768]{2,1,0:T(2,128)(2,1)S(1)}, u32[]{:S(2)}, u32[]{:S(2)}) collective-permute-start(bf16[8,2,768]{2,1,0:T(2,128)(2,1)S(1)} %pad_maximum_fusion), channel_id=1, source_target_pairs={{0,1},{1,2},{2,3},{4,5},{5,6},{6,7},{8,9},{9,10},{10,11},{12,13},{... | collective-permute-start | bytes 73736 | tf_op jit(solution)/shard_map/ppermute | solution.py:94
  34.9 4.9 %collective-permute-start.3 = (bf16[8,2,768]{2,1,0:T(2,128)(2,1)S(1)}, bf16[8,2,768]{2,1,0:T(2,128)(2,1)S(1)}, u32[]{:S(2)}, u32[]{:S(2)}) collective-permute-start(bf16[8,2,768]{2,1,0:T(2,128)(2,1)S(1)} %pad_maximum_fusion.1), channel_id=1, source_target_pairs={{1,0},{2,1},{3,2},{5,4},{6,5},{7,6},{9,8},{10,9},{11,10},{13,12},{... | collective-permute-start | bytes 73736 | tf_op jit(solution)/shard_map/ppermute | solution.py:94
  36.2 8.3 %copy-start.4 = (bf16[8,2,768]{2,1,0:T(2,128)(2,1)}, bf16[8,2,768]{2,1,0:T(2,128)(2,1)S(1)}, u32[]{:S(2)}) copy-start(bf16[8,2,768]{2,1,0:T(2,128)(2,1)S(1)} %collective-permute-done.2.west_ref) | copy-start | bytes 73732
  39.8 4.7 %copy-start.5 = (bf16[8,2,768]{2,1,0:T(2,128)(2,1)}, bf16[8,2,768]{2,1,0:T(2,128)(2,1)S(1)}, u32[]{:S(2)}) copy-start(bf16[8,2,768]{2,1,0:T(2,128)(2,1)S(1)} %collective-permute-done.3.east_ref) | copy-start | bytes 73732
  40.8 12.9 %all-to-all-start.1 = ((bf16[4,256,384]{2,1,0:T(8,128)(2,1)}), bf16[4,256,384]{2,1,0:T(8,128)(2,1)S(1)}, u32[]{:S(2)}, u32[]{:S(2)}) async-start(bf16[4,256,384]{2,1,0:T(8,128)(2,1)} %broadcast_in_dim.2), calls=%async_computation.1 | async-start | bytes 1572864 | tf_op jit(solution)/shard_map/all_to_all | solution.py:77
  53.7 12.0 %copy-start = (bf16[4,256,384]{2,1,0:T(8,128)(2,1)}, bf16[4,256,384]{2,1,0:T(8,128)(2,1)S(1)}, u32[]{:S(2)}) copy-start(bf16[4,256,384]{2,1,0:T(8,128)(2,1)S(1)} %all-to-all-done.1) | copy-start | bytes 2359300
  53.7 12.0 %collective-permute-start.4 = (bf16[1024,384]{1,0:T(8,128)(2,1)S(1)}, bf16[1024,384]{1,0:T(8,128)(2,1)S(1)}, u32[]{:S(2)}, u32[]{:S(2)}) collective-permute-start(bf16[1024,384]{1,0:T(8,128)(2,1)S(1)} %bitcast.4), channel_id=1, source_target_pairs={{0,4},{4,0},{8,12},{12,8},{16,20},{20,16},{24,28},{28,24},{32,36},... | collective-permute-start | bytes 2359304 | tf_op jit(solution)/shard_map/ppermute | solution.py:372
  65.6 0.9 copy-start.3

commit v3 on v2

--- a/solution.py
+++ b/solution.py
@@ -18,7 +18,7 @@
 EPS = 1e-06
 SCORE_SCALE = 1.0 / math.sqrt(HDIM) * math.log2(math.e)
 SAFE_SCORE = 96.0
-TILE = 1024
+TILES = (1024, 1024)
 
 F32 = jnp.float32
 BF16 = jnp.bfloat16
@@ -125,7 +125,7 @@
 
 
 def front_kernel(
-    field_ref, top_ref, bottom_ref, west_ref, east_ref, gain_ref, conv_ref, query_ref, mix_ref,
+    _, field_ref, top_ref, bottom_ref, west_ref, east_ref, gain_ref, conv_ref, query_ref, mix_ref,
     acc_ref, q_ref, done_ref, cells, outer, centre, packed, acc, queries, sems,
 ):
     span_p, span_e = field_ref.shape[0], field_ref.shape[1]
@@ -166,7 +166,7 @@
     done_ref[...] = jnp.zeros_like(done_ref)
 
 
-def front(field, top, bottom, west, east, gain, conv_weight, query_weight, mix_weight):
+def front(edges, field, top, bottom, west, east, gain, conv_weight, query_weight, mix_weight):
     span_p, span_e = field.shape[0], field.shape[1]
     vmem = pl.BlockSpec(memory_space=pltpu.VMEM)
     rows, width = span_p + 2, (span_e + 2) * LAYERS
@@ -177,7 +177,7 @@
             jax.ShapeDtypeStruct((rows * width, C), BF16),
             jax.ShapeDtypeStruct((8, LANES), BF16),
         ],
-        in_specs=[vmem] * 9,
+        in_specs=[pl.BlockSpec(memory_space=pltpu.SMEM)] + [vmem] * 9,
         out_specs=[pl.BlockSpec(memory_space=pltpu.HBM)] * 2 + [vmem],
         scratch_shapes=[
             pltpu.VMEM((rows + 2, width + 2 * LAYERS, LANES), F32),
@@ -193,7 +193,7 @@
             flops=6_000_000_000, bytes_accessed=5_000_000, transcendentals=400_000
         ),
         name="front",
-    )(field, top, bottom, west, east, gain, conv_weight, query_weight, mix_weight)
+    )(edges, field, top, bottom, west, east, gain, conv_weight, query_weight, mix_weight)
 
 
 def prepare_tokens(kv_refs, keys, values):
@@ -242,24 +242,23 @@
 
 
 def back_kernel(
-    edge_ref, _, acc_ref, q_ref, kv_ref, other_ref, field_in, noise_in, gain_ref, conv_ref,
-    query_ref, mix_ref, out_ref, result_ref, keys, values, attended, second, stream, outer, centre,
-    packed, flat, acc, queries, field_ref, noise_ref, sems,
+    edge_ref, _, acc_ref, q_ref, kv_ref, other_ref, field_in, noise_in, gain_in, conv_in,
+    query_in, mix_in, out_in, result_ref, keys, values, attended, second, stream, outer, centre,
+    packed, flat, acc, queries, field_ref, noise_ref, gain_ref,
+    conv_ref, query_ref, mix_ref, out_ref, sems,
 ):
     span_p, span_e = field_ref.shape[0], field_ref.shape[1]
     width, inner = (span_e + 2) * LAYERS, span_e * LAYERS
     q_copy = pltpu.make_async_copy(q_ref, queries, sems.at[0])
     acc_copy = pltpu.make_async_copy(acc_ref, acc, sems.at[1])
-    late = [
-        pltpu.make_async_copy(field_in, field_ref, sems.at[2]),
-        pltpu.make_async_copy(noise_in, noise_ref, sems.at[3]),
+    pairs = [
+        (gain_in, gain_ref), (conv_in, conv_ref), (query_in, query_ref), (mix_in, mix_ref),
+        (out_in, out_ref), (field_in, field_ref), (noise_in, noise_ref),
     ]
+    late = [pltpu.make_async_copy(a, b, sems.at[2 + i]) for i, (a, b) in enumerate(pairs)]
     for copy in [q_copy, acc_copy] + late:
         copy.start()
-    gain = widened(gain_ref[1:2, :])
     largest = prepare_tokens([kv_ref, other_ref], keys, values)
-    pack_weight(conv_ref, 1, packed)
-
     def attend_rows(source, block, start, rows):
         q = jnp.transpose(source[pl.ds(start, rows), :])
         fine = within(q, largest[block])
@@ -272,20 +271,24 @@
         pl.when(jnp.logical_not(fine))(lambda: go(False))
 
     def attend_all(source, block, count):
-        tiles = count // TILE
+        size = TILES[block]
+        tiles = count // size
 
         @pl.loop(0, tiles)
         def _(tile):
-            attend_rows(source, block, pl.multiple_of(tile * TILE, TILE), TILE)
-
-        rest = count - tiles * TILE
+            attend_rows(source, block, pl.multiple_of(tile * size, size), size)
+
+        rest = count - tiles * size
         if rest:
             rest = -(-rest // LANES) * LANES
             attend_rows(source, block, count - rest, rest)
 
     q_copy.wait()
     attend_all(queries, 0, (span_p + 2) * width)
-    acc_copy.wait()
+    for copy in [acc_copy] + late:
+        copy.wait()
+    gain = widened(gain_ref[1:2, :])
+    pack_weight(conv_ref, 1, packed)
     for row in range(span_p + 2):
         branch = dot(attended[row * width : (row + 1) * width, :], out_ref[0])
         new = acc[row] + branch
@@ -302,8 +305,6 @@
             second[(row - 1) * inner : row * inner, :] = q.astype(BF16)
 
     attend_all(second, 1, span_p * inner)
-    for copy in late:
-        copy.wait()
     for row in range(span_p):
         branch = conv_branch(outer, centre, row, inner, packed, mix_ref[1])
         new = stream[row] + branch + dot(attended[row * inner : (row + 1) * inner, :], out_ref[1])
@@ -327,8 +328,7 @@
         in_specs=[pl.BlockSpec(memory_space=pltpu.SMEM), pl.BlockSpec(memory_space=pl.ANY)]
         + [pl.BlockSpec(memory_space=pltpu.HBM)] * 2
         + [vmem] * 2
-        + [pl.BlockSpec(memory_space=pl.ANY)] * 2
-        + [vmem] * 5,
+        + [pl.BlockSpec(memory_space=pl.ANY)] * 7,
         out_specs=vmem,
         scratch_shapes=[
             pltpu.VMEM((BLOCKS, tokens, C), BF16),
@@ -344,9 +344,14 @@
             pltpu.VMEM((rows * width, C), BF16),
             pltpu.VMEM(field.shape, BF16),
             pltpu.VMEM(field.shape, BF16),
-            pltpu.SemaphoreType.DMA((4,)),
+            pltpu.VMEM(gain.shape, F32),
+            pltpu.VMEM(conv_weight.shape, BF16),
+            pltpu.VMEM(query_weight.shape, BF16),
+            pltpu.VMEM(mix_weight.shape, BF16),
+            pltpu.VMEM(out_weight.shape, BF16),
+            pltpu.SemaphoreType.DMA((9,)),
         ],
-        compiler_params=pltpu.CompilerParams(vmem_limit_bytes=60 * 1024 * 1024),
+        compiler_params=pltpu.CompilerParams(vmem_limit_bytes=62_259_200),
         cost_estimate=pl.CostEstimate(
             flops=20_000_000_000, bytes_accessed=6_000_000, transcendentals=21_000_000
         ),
@@ -355,8 +360,8 @@
 
 
 def tokens_and_front(
-    coarse_latent, particle_type, type_table, kv_weight, field, gain, conv_weight, query_weight,
-    mix_weight,
+    edges, coarse_latent, particle_type, type_table, kv_weight, field, gain, conv_weight,
+    query_weight, mix_weight,
 ):
     local = local_tokens(coarse_latent, particle_type, type_table, kv_weight, len(YZ_GROUPS[0]))
     top, bottom = halo_phi(field)
@@ -364,7 +369,7 @@
     kv = exchange(local, YZ_GROUPS)
     kv, west, east = lax.optimization_barrier((kv, west, east))
     acc, q, done = front(
-        field, top, bottom, west, east, gain, conv_weight, query_weight, mix_weight
+        edges, field, top, bottom, west, east, gain, conv_weight, query_weight, mix_weight
     )
     copies = jnp.broadcast_to(kv[None], (len(X_GROUPS[0]),) + kv.shape)
     kv = exchange(copies, X_GROUPS)
@@ -386,12 +391,12 @@
     mix_weight,
     out_weight,
 ):
-    kv, other, acc, q, done = tokens_and_front(
-        coarse_latent, particle_type, type_table, kv_weight, noisy_field, norm_gain, conv_weight,
-        query_weight, mix_weight,
-    )
     band = lax.axis_index("eta")
     edges = jnp.stack([band == 0, band == lax.axis_size("eta") - 1]).astype(jnp.int32)
+    kv, other, acc, q, done = tokens_and_front(
+        edges, coarse_latent, particle_type, type_table, kv_weight, noisy_field, norm_gain,
+        conv_weight, query_weight, mix_weight,
+    )
     return back(
         edges, done, acc, q, kv, other, noisy_field, noise_draw, norm_gain, conv_weight, query_weight,
         mix_weight, out_weight,

time: 101 us -> 98.7 us (0.977)
  Pallas kernels: 43.3 us -> 41.3 us
    pallas_call x1, Pallas kernels: 32.1 us -> 30.1 us  [back(): pl.pallas_call(back_kernel, out_shape=jax.ShapeDtypeStruct(field.shape, B...]
where the time goes in v3:
time: 98.7 us; the launch traced here: 97.1 us
  Pallas kernels  41.3 us (42%)
  starting transfers between devices  40.9 us (41%)
  waiting for transfers between devices  10.2 us (10%)
  local copies, waits for them, and re-layouts  3.8 us (4%)
    pallas_call x1, Pallas kernels, back(): pl.pallas_call(back_kernel, out_shape=jax.ShapeDtypeStruct(field.shape, B...  30.1 us
    all_to_all x2, starting transfers between devices, exchange(): lax.all_to_all(copies, 'phi', 0, 0, tiled=True, axis_index_groups=groups)  19.9 us
    ppermute x1, starting transfers between devices, tokens_and_front(): lax.ppermute(kv, 'phi', [(i, i ^ 1) for i in range(lax.axis_size('phi'))])  10 us
    pallas_call x1, Pallas kernels, front(): pl.pallas_call(front_kernel, out_shape=[jax.ShapeDtypeStruct((rows, width...  9.17 us
    ppermute x2, starting transfers between devices, halo_eta(): return (lax.ppermute(west, 'eta', right), lax.ppermute(east, 'eta', left))  4.69 us
    ppermute x1, starting transfers between devices, halo_phi(): lax.ppermute(field[-2:], 'phi', up)  4.39 us
    ppermute x2, waiting for transfers between devices, halo_eta(): return (lax.ppermute(west, 'eta', right), lax.ppermute(east, 'eta', left))  3.57 us
    ppermute x1, waiting for transfers between devices, halo_phi(): lax.ppermute(field[:2], 'phi', down)  3.44 us
  transfers between devices with their start and end apart: 7, of which 4 were waited for; matrix products, arithmetic and copies ran while one was open for 3% of the time, Pallas kernels for 9%

profile of v3, /device:TPU:1, one launch (start us, length us, event | category | flops | bytes accessed | tf_op | source)
XLA Modules:
  0.0 97.1 jit_solution(14600187254251391967)
XLA Ops:
  0.0 2.0 %tokens.1 = bf16[16,16,384]{2,1,0:T(8,128)(2,1)} custom-call(s32[16]{0:T(128)} %type_ref.1, bf16[16,512]{1,0:T(8,128)(2,1)} %latent_ref.1, bf16[8,512]{1,0:T(8,128)(2,1)} %table_ref.1, bf16[512,384]{1,0:T(8,128)(2,1)} %weight_ref.1), custom_call_target="tpu_custom_call" | custom-call | flops 6000000 | bytes 700000 | tf_op jit(solution)/shard_map/tokens/pallas_call | solution.py:52
  2.0 16.2 %all-to-all-start = ((bf16[16,16,384]{2,1,0:T(8,128)(2,1)}), bf16[16,16,384]{2,1,0:T(8,128)(2,1)S(1)}, u32[]{:S(2)}, u32[]{:S(2)}) async-start(bf16[16,16,384]{2,1,0:T(8,128)(2,1)} %tokens.1), calls=%async_computation | async-start | bytes 393216 | tf_op jit(solution)/shard_map/all_to_all | solution.py:77
  18.2 1.1 %fusion.1 = (bf16[2,64,768]{2,1,0:T(8,128)(2,1)S(1)}, bf16[2,64,768]{2,1,0:T(8,128)(2,1)S(1)}) fusion(bf16[4,64,768]{2,1,0:T(8,128)(2,1)} %field_in.1), kind=kLoop, calls=%fused_computation.4 | loop fusion | bytes 786432 | tf_op jit(solution)/shard_map/slice | solution.py:85
  19.3 4.4 %collective-permute-start = (bf16[2,64,768]{2,1,0:T(8,128)(2,1)S(1)}, bf16[2,64,768]{2,1,0:T(8,128)(2,1)S(1)}, u32[]{:S(2)}, u32[]{:S(2)}) collective-permute-start(bf16[2,64,768]{2,1,0:T(8,128)(2,1)S(1)} %get-tuple-element.23), channel_id=1, source_target_pairs={{0,4},{4,8},{8,12},{12,16},{16,20},{20,24},{24,28},{28,32},{32,36}... | collective-permute-start | bytes 589832 | tf_op jit(solution)/shard_map/ppermute | solution.py:85
  23.7 1.9 %collective-permute-start.1 = (bf16[2,64,768]{2,1,0:T(8,128)(2,1)S(1)}, bf16[2,64,768]{2,1,0:T(8,128)(2,1)S(1)}, u32[]{:S(2)}, u32[]{:S(2)}) collective-permute-start(bf16[2,64,768]{2,1,0:T(8,128)(2,1)S(1)} %get-tuple-element.24), channel_id=1, source_target_pairs={{4,0},{8,4},{12,8},{16,12},{20,16},{24,20},{28,24},{32,28},{36,32}... | collective-permute-start | bytes 589832 | tf_op jit(solution)/shard_map/ppermute | solution.py:85
  25.6 0.8 fusion
  26.5 1.4 %collective-permute-done.top_ref = bf16[2,64,768]{2,1,0:T(8,128)(2,1)S(1)} collective-permute-done((bf16[2,64,768]{2,1,0:T(8,128)(2,1)S(1)}, bf16[2,64,768]{2,1,0:T(8,128)(2,1)S(1)}, u32[]{:S(2)}, u32[]{:S(2)}) %collective-permute-start) | collective-permute-done | bytes 196640 | tf_op jit(solution)/shard_map/ppermute | solution.py:85
  27.9 3.4 %collective-permute-done.1.bottom_ref = bf16[2,64,768]{2,1,0:T(8,128)(2,1)S(1)} collective-permute-done((bf16[2,64,768]{2,1,0:T(8,128)(2,1)S(1)}, bf16[2,64,768]{2,1,0:T(8,128)(2,1)S(1)}, u32[]{:S(2)}, u32[]{:S(2)}) %collective-permute-start.1) | collective-permute-done | bytes 196640 | tf_op jit(solution)/shard_map/ppermute | solution.py:85
  31.4 3.4 %collective-permute-start.2 = (bf16[8,2,768]{2,1,0:T(2,128)(2,1)S(1)}, bf16[8,2,768]{2,1,0:T(2,128)(2,1)S(1)}, u32[]{:S(2)}, u32[]{:S(2)}) collective-permute-start(bf16[8,2,768]{2,1,0:T(2,128)(2,1)S(1)} %pad_maximum_fusion), channel_id=1, source_target_pairs={{0,1},{1,2},{2,3},{4,5},{5,6},{6,7},{8,9},{9,10},{10,11},{12,13},{... | collective-permute-start | bytes 73736 | tf_op jit(solution)/shard_map/ppermute | solution.py:94
  34.9 1.3 %collective-permute-start.3 = (bf16[8,2,768]{2,1,0:T(2,128)(2,1)S(1)}, bf16[8,2,768]{2,1,0:T(2,128)(2,1)S(1)}, u32[]{:S(2)}, u32[]{:S(2)}) collective-permute-start(bf16[8,2,768]{2,1,0:T(2,128)(2,1)S(1)} %pad_maximum_fusion.1), channel_id=1, source_target_pairs={{1,0},{2,1},{3,2},{5,4},{6,5},{7,6},{9,8},{10,9},{11,10},{13,12},{... | collective-permute-start | bytes 73736 | tf_op jit(solution)/shard_map/ppermute | solution.py:94
  36.2 0.0 collective-permute-done.2.west_ref
  36.2 0.0 copy-start.4
  36.2 3.6 %collective-permute-done.3.east_ref = bf16[8,2,768]{2,1,0:T(2,128)(2,1)S(1)} collective-permute-done((bf16[8,2,768]{2,1,0:T(2,128)(2,1)S(1)}, bf16[8,2,768]{2,1,0:T(2,128)(2,1)S(1)}, u32[]{:S(2)}, u32[]{:S(2)}) %collective-permute-start.3) | collective-permute-done | bytes 24608 | tf_op jit(solution)/shard_map/ppermute | solution.py:94
  39.8 0.0 all-to-all-done
  39.8 1.0 broadcast_in_dim.2
  40.8 3.7 %all-to-all-start.1 = ((bf16[4,256,384]{2,1,0:T(8,128)(2,1)}), bf16[4,256,384]{2,1,0:T(8,128)(2,1)S(1)}, u32[]{:S(2)}, u32[]{:S(2)}) async-start(bf16[4,256,384]{2,1,0:T(8,128)(2,1)} %broadcast_in_dim.2), calls=%async_computation.1 | async-start | bytes 1572864 | tf_op jit(solution)/shard_map/all_to_all | solution.py:77
  44.5 0.6 add_convert_fusion._.edge_ref
  45.0 0.0 copy-done.2
  45.0 9.2 %front.1 = (f32[6,528,96]{2,1,0:T(8,128)}, bf16[3168,96]{1,0:T(8,128)(2,1)}, bf16[8,128]{1,0:T(8,128)(2,1)}) custom-call(s32[2]{0:T(128)} %add_convert_fusion._.edge_ref, bf16[4,64,768]{2,1,0:T(8,128)(2,1)} %field_in.1, bf16[2,64,768]{2,1,0:T(8,128)(2,1)} %copy-done.1, bf16[2,64,768]{2,1,0:T(8,128)(2,1)} %copy-done.2, bf16[8,2,768]{2,1,0:T(2,128)(2,1)} %copy-done.4, ...), custom_call_target="tpu_custom_call" | custom-call | flops 6000000000 | bytes 5000000 | tf_op jit(solution)/shard_map/front/pallas_call | solution.py:173
  54.2 0.0 all-to-all-done.1
  54.2 10.0 %collective-permute-start.4 = (bf16[1024,384]{1,0:T(8,128)(2,1)S(1)}, bf16[1024,384]{1,0:T(8,128)(2,1)S(1)}, u32[]{:S(2)}, u32[]{:S(2)}) collective-permute-start(bf16[1024,384]{1,0:T(8,128)(2,1)S(1)} %bitcast.4), channel_id=1, source_target_pairs={{0,4},{4,0},{8,12},{12,8},{16,20},{20,16},{24,28},{28,24},{32,36},... | collective-permute-start | bytes 2359304 | tf_op jit(solution)/shard_map/ppermute | solution.py:377
  64.3 1.7 %collective-permute-done.4.other_ref = bf16[1024,384]{1,0:T(8,128)(2,1)S(1)} collective-permute-done((bf16[1024,384]{1,0:T(8,128)(2,1)S(1)}, bf16[1024,384]{1,0:T(8,128)(2,1)S(1)}, u32[]{:S(2)}, u32[]{:S(2)}) %collective-permute-start.4) | collective-permute-done | bytes 786464 | tf_op jit(solution)/shard_map/ppermute | solution.py:377
  66.0 0.9 copy-done.3
  66.9 30.1 %back.1 = bf16[4,64,768]{2,1,0:T(8,128)(2,1)} custom-call(s32[2]{0:T(128)} %add_convert_fusion._.edge_ref, bf16[8,128]{1,0:T(8,128)(2,1)} %get-tuple-element.17._, f32[6,528,96]{2,1,0:T(8,128)} %get-tuple-element.18.acc_ref, bf16[3168,96]{1,0:T(8,128)(2,1)} %get-tuple-element.19.q_ref, bf16[1024,384]{1,0:T(8,128)(2,1)} %bitcast.5, ...), custom_call_target="tpu_custom_call" | custom-call | flops 20000000000 | bytes 6000000 | tf_op jit(solution)/shard_map/back/pallas_call | solution.py:325
  (13 shorter events, 0.1 us)
Async XLA Ops:
  2.0 37.8 %all-to-all-start = ((bf16[16,16,384]{2,1,0:T(8,128)(2,1)}), bf16[16,16,384]{2,1,0:T(8,128)(2,1)S(1)}, u32[]{:S(2)}, u32[]{:S(2)}) async-start(bf16[16,16,384]{2,1,0:T(8,128)(2,1)} %tokens.1), calls=%async_computation | async-start | bytes 393216 | tf_op jit(solution)/shard_map/all_to_all | solution.py:77
  19.3 8.6 %collective-permute-start = (bf16[2,64,768]{2,1,0:T(8,128)(2,1)S(1)}, bf16[2,64,768]{2,1,0:T(8,128)(2,1)S(1)}, u32[]{:S(2)}, u32[]{:S(2)}) collective-permute-start(bf16[2,64,768]{2,1,0:T(8,128)(2,1)S(1)} %get-tuple-element.23), channel_id=1, source_target_pairs={{0,4},{4,8},{8,12},{12,16},{16,20},{20,24},{24,28},{28,32},{32,36}... | collective-permute-start | bytes 589832 | tf_op jit(solution)/shard_map/ppermute | solution.py:85
  23.7 7.7 %collective-permute-start.1 = (bf16[2,64,768]{2,1,0:T(8,128)(2,1)S(1)}, bf16[2,64,768]{2,1,0:T(8,128)(2,1)S(1)}, u32[]{:S(2)}, u32[]{:S(2)}) collective-permute-start(bf16[2,64,768]{2,1,0:T(8,128)(2,1)S(1)} %get-tuple-element.24), channel_id=1, source_target_pairs={{4,0},{8,4},{12,8},{16,12},{20,16},{24,20},{28,24},{32,28},{36,32}... | collective-permute-start | bytes 589832 | tf_op jit(solution)/shard_map/ppermute | solution.py:85
  27.9 17.1 %copy-start.1 = (bf16[2,64,768]{2,1,0:T(8,128)(2,1)}, bf16[2,64,768]{2,1,0:T(8,128)(2,1)S(1)}, u32[]{:S(2)}) copy-start(bf16[2,64,768]{2,1,0:T(8,128)(2,1)S(1)} %collective-permute-done.top_ref) | copy-start | bytes 589828
  31.4 13.7 %copy-start.2 = (bf16[2,64,768]{2,1,0:T(8,128)(2,1)}, bf16[2,64,768]{2,1,0:T(8,128)(2,1)S(1)}, u32[]{:S(2)}) copy-start(bf16[2,64,768]{2,1,0:T(8,128)(2,1)S(1)} %collective-permute-done.1.bottom_ref) | copy-start | bytes 589828
  31.4 4.8 %collective-permute-start.2 = (bf16[8,2,768]{2,1,0:T(2,128)(2,1)S(1)}, bf16[8,2,768]{2,1,0:T(2,128)(2,1)S(1)}, u32[]{:S(2)}, u32[]{:S(2)}) collective-permute-start(bf16[8,2,768]{2,1,0:T(2,128)(2,1)S(1)} %pad_maximum_fusion), channel_id=1, source_target_pairs={{0,1},{1,2},{2,3},{4,5},{5,6},{6,7},{8,9},{9,10},{10,11},{12,13},{... | collective-permute-start | bytes 73736 | tf_op jit(solution)/shard_map/ppermute | solution.py:94
  34.9 4.9 %collective-permute-start.3 = (bf16[8,2,768]{2,1,0:T(2,128)(2,1)S(1)}, bf16[8,2,768]{2,1,0:T(2,128)(2,1)S(1)}, u32[]{:S(2)}, u32[]{:S(2)}) collective-permute-start(bf16[8,2,768]{2,1,0:T(2,128)(2,1)S(1)} %pad_maximum_fusion.1), channel_id=1, source_target_pairs={{1,0},{2,1},{3,2},{5,4},{6,5},{7,6},{9,8},{10,9},{11,10},{13,12},{... | collective-permute-start | bytes 73736 | tf_op jit(solution)/shard_map/ppermute | solution.py:94
  36.2 8.8 %copy-start.4 = (bf16[8,2,768]{2,1,0:T(2,128)(2,1)}, bf16[8,2,768]{2,1,0:T(2,128)(2,1)S(1)}, u32[]{:S(2)}) copy-start(bf16[8,2,768]{2,1,0:T(2,128)(2,1)S(1)} %collective-permute-done.2.west_ref) | copy-start | bytes 73732
  39.8 5.2 %copy-start.5 = (bf16[8,2,768]{2,1,0:T(2,128)(2,1)}, bf16[8,2,768]{2,1,0:T(2,128)(2,1)S(1)}, u32[]{:S(2)}) copy-start(bf16[8,2,768]{2,1,0:T(2,128)(2,1)S(1)} %collective-permute-done.3.east_ref) | copy-start | bytes 73732
  40.8 13.5 %all-to-all-start.1 = ((bf16[4,256,384]{2,1,0:T(8,128)(2,1)}), bf16[4,256,384]{2,1,0:T(8,128)(2,1)S(1)}, u32[]{:S(2)}, u32[]{:S(2)}) async-start(bf16[4,256,384]{2,1,0:T(8,128)(2,1)} %broadcast_in_dim.2), calls=%async_computation.1 | async-start | bytes 1572864 | tf_op jit(solution)/shard_map/all_to_all | solution.py:77
  54.2 11.8 %copy-start = (bf16[4,256,384]{2,1,0:T(8,128)(2,1)}, bf16[4,256,384]{2,1,0:T(8,128)(2,1)S(1)}, u32[]{:S(2)}) copy-start(bf16[4,256,384]{2,1,0:T(8,128)(2,1)S(1)} %all-to-all-done.1) | copy-start | bytes 2359300
  54.2 11.7 %collective-permute-start.4 = (bf16[1024,384]{1,0:T(8,128)(2,1)S(1)}, bf16[1024,384]{1,0:T(8,128)(2,1)S(1)}, u32[]{:S(2)}, u32[]{:S(2)}) collective-permute-start(bf16[1024,384]{1,0:T(8,128)(2,1)S(1)} %bitcast.4), channel_id=1, source_target_pairs={{0,4},{4,0},{8,12},{12,8},{16,20},{20,16},{24,28},{28,24},{32,36},... | collective-permute-start | bytes 2359304 | tf_op jit(solution)/shard_map/ppermute | solution.py:377
  66.0 0.9 copy-start.3
